TPU v7x, 128 devices: a whole 4x4x4 slice. The times are simulated.
128 devices in a mesh: expert: 32 (over y_hi, z, x), width: 4 (over y_lo, core).
Axes of the slice: x: 4, y: 4 (y_hi: 2, y_lo: 2; y = y_hi * 2 + y_lo), z: 4, core: 2. Of those that a mesh axis runs over, the one named last changes fastest.
Arguments:
- tokens: bfloat16 [4096, 2880], P('expert', 'width'), may hold values from -6 to 6
- grad_out: bfloat16 [4096, 2880], P('expert', 'width'), may hold values from -6 to 6
- routes: int32 [4096, 4], P('expert'), may hold values from 0 to 127, all different within a row; in each aligned block of 128 rows (0 to 127, 128 to 255, ...) at most 5 rows name the same one
- gates: float32 [4096, 4], P('expert'), may hold values from 0.05 to 1
- ranks: int32 [128], P('expert'), may hold values from 64 to 512
- w_gate: bfloat16 [2880, 2880], P('expert', 'width'), may hold values from -0.109375 to 0.109375
- w_up: bfloat16 [2880, 2880], P('expert', 'width'), may hold values from -0.109375 to 0.109375
- w_down: bfloat16 [2880, 2880], P('width', 'expert'), may hold values from -0.109375 to 0.109375
- delta_in: bfloat16 [128, 2880, 512], P('expert', 'width'), may hold values from -0.109375 to 0.109375
- delta_out: bfloat16 [128, 512, 2, 2880], P('expert', None, None, 'width'), may hold values from -0.25 to 0.25
Outputs:
- grad_tokens: bfloat16 [4096, 2880], P('expert', 'width')
- grad_gate: bfloat16 [2880, 2880], P('expert', 'width')
- grad_up: bfloat16 [2880, 2880], P('expert', 'width')
- grad_down: bfloat16 [2880, 2880], P('width', 'expert')
- grad_delta_in: bfloat16 [128, 2880, 512], P('expert', 'width')
- grad_delta_out: bfloat16 [128, 512, 2, 2880], P('expert', None, None, 'width')
Inputs may be any that keep to these rules, and one draw needn't show every extreme that they name: `routes`: each row names 4 different experts; among the 128 rows of one index of the expert axis (aligned blocks) no expert is named by more than 5 rows, a bound that some block reaches in every draw.
All inputs are finite; a program needn't handle non-finite values.
Results may differ from a plain program's by a relative error of at most 0.03.
Values may be sent and summed in bfloat16 or wider, within the bound.
No kernel may reach another device: no remote copies, remote signals or barrier semaphores. Data moves between devices by JAX's collectives and lax.ppermute only.
A program may use at most 128 MiB of HBM per device.

v0:
```python
import jax
import jax.numpy as jnp
from jax import lax
from jax.sharding import PartitionSpec as P


def local(tokens, grad_out, routes, gates, ranks, w_gate, w_up, w_down, delta_in, delta_out):
    precise = lax.Precision.HIGHEST
    over_rows = (((0,), (0,)), ((), ()))
    over_cols = (((1,), (1,)), ((), ()))
    expert_count = lax.axis_size("expert")
    token_rows, part_width = tokens.shape
    top_count = routes.shape[1]
    local_experts = delta_in.shape[0]
    rank_max = delta_in.shape[2]
    hidden_part = w_gate.shape[1]
    experts = local_experts * expert_count
    capacity = max(2, 5 * token_rows * top_count // (4 * experts))
    slot_count = experts * capacity
    whole_x, whole_dy = (
        lax.all_gather(tokens, "width", axis=1, tiled=True),
        lax.all_gather(grad_out, "width", axis=1, tiled=True),
    )
    weight_both = jnp.concatenate([w_gate, w_up], axis=1)
    full_both = lax.all_gather(weight_both, "expert", axis=0, tiled=True)
    base_both = jnp.dot(whole_x, full_both, preferred_element_type=jnp.float32)
    base_both = base_both.astype(jnp.bfloat16)
    columns = whole_dy
    down_grad = lax.dot_general(
        columns,
        lax.all_gather(w_down, "expert", axis=1, tiled=True),
        over_cols,
        preferred_element_type=jnp.float32,
    )
    flat_routes = routes.reshape(-1)
    expert_ids = lax.broadcasted_iota(jnp.int32, (1, experts), 1)
    onehot = (flat_routes[:, None] == expert_ids).astype(jnp.int32)
    before = jnp.cumsum(onehot, axis=0) - onehot
    slot_index = jnp.sum(before * onehot, axis=1)
    target = flat_routes * capacity + slot_index
    slot_ids = lax.broadcasted_iota(jnp.int32, (slot_count, 1), 0)
    slot_map = (target[None, :] == slot_ids).astype(jnp.float32)
    weighted = (
        (slot_map * gates.reshape(1, -1)).reshape(slot_count, token_rows, top_count).sum(axis=2)
    )
    picker = slot_map.reshape(slot_count, token_rows, top_count).sum(axis=2).astype(jnp.bfloat16)
    moved_rows = jnp.dot(
        picker, jnp.concatenate([tokens, base_both], axis=1), preferred_element_type=jnp.float32
    ).astype(jnp.bfloat16)
    pair_down = jnp.dot(weighted, down_grad, precision=precise).astype(jnp.bfloat16)
    outgoing = jnp.concatenate([moved_rows, pair_down], axis=1).reshape(
        expert_count, local_experts, capacity, -1
    )
    incoming = lax.all_to_all(outgoing, "expert", split_axis=0, concat_axis=2, tiled=True)
    incoming = incoming.reshape(local_experts, expert_count * capacity, -1)
    rows_x = incoming[:, :, :part_width]
    base_in = incoming[:, :, part_width : part_width + 2 * hidden_part].astype(jnp.float32)
    base_in = base_in.reshape(local_experts, -1, 2, hidden_part)
    down_in = incoming[:, :, part_width + 2 * hidden_part :].astype(jnp.float32)
    rank_mask = (
        lax.broadcasted_iota(jnp.int32, (local_experts, 1, rank_max), 2) < ranks[:, None, None]
    ).astype(jnp.float32)
    partial_low = jnp.einsum("erd,edk->erk", rows_x, delta_in, preferred_element_type=jnp.float32)
    low_rank = (
        lax.psum(partial_low.astype(jnp.bfloat16), "width").astype(jnp.float32) * rank_mask
    ).astype(jnp.bfloat16)
    pre_act = base_in + jnp.einsum(
        "erk,ekcf->ercf", low_rank, delta_out, preferred_element_type=jnp.float32
    )
    activation = pre_act[:, :, 0]
    up_value = pre_act[:, :, 1]
    sigmoid_act = jax.nn.sigmoid(activation)
    swish_value = activation * sigmoid_act
    hidden = (swish_value * up_value).astype(jnp.bfloat16)
    grad_act = down_in * up_value * sigmoid_act * (1.0 + activation * (1.0 - sigmoid_act))
    grad_upper = down_in * swish_value
    pair_grad = jnp.stack([grad_act, grad_upper], axis=2).astype(jnp.bfloat16)
    grad_delta_out = jnp.einsum(
        "erk,ercf->ekcf", low_rank, pair_grad, preferred_element_type=jnp.float32
    ).astype(jnp.bfloat16)
    partial_back = jnp.einsum(
        "ercf,ekcf->erk", pair_grad, delta_out, preferred_element_type=jnp.float32
    )
    low_grad = (
        lax.psum(partial_back.astype(jnp.bfloat16), "width").astype(jnp.float32) * rank_mask
    ).astype(jnp.bfloat16)
    grad_delta_in = jnp.einsum(
        "erd,erk->edk", rows_x, low_grad, preferred_element_type=jnp.float32
    ).astype(jnp.bfloat16)
    back_rows = jnp.einsum(
        "erk,edk->erd", low_grad, delta_in, preferred_element_type=jnp.float32
    ).astype(jnp.bfloat16)
    returning = jnp.concatenate(
        [back_rows, hidden, pair_grad.reshape(local_experts, -1, 2 * hidden_part)], axis=2
    )
    returning = returning.reshape(local_experts, expert_count, capacity, -1)
    arrived = lax.all_to_all(returning, "expert", split_axis=1, concat_axis=0, tiled=True).reshape(
        slot_count, -1
    )
    back_in = arrived[:, :part_width]
    hidden_back = arrived[:, part_width : part_width + hidden_part].astype(jnp.float32)
    grads_back = arrived[:, part_width + hidden_part :]
    token_back = lax.dot_general(picker, back_in, over_rows, preferred_element_type=jnp.float32)
    mixed_hidden = lax.dot_general(weighted, hidden_back, over_rows, precision=precise).astype(
        jnp.bfloat16
    )
    summed = lax.dot_general(
        picker, grads_back, over_rows, preferred_element_type=jnp.float32
    ).astype(jnp.bfloat16)
    columns = whole_x
    base_share = lax.psum_scatter(
        lax.dot_general(columns, summed, over_rows, preferred_element_type=jnp.float32).astype(
            jnp.bfloat16
        ),
        "expert",
        scatter_dimension=0,
        tiled=True,
    ).astype(jnp.float32)
    columns = whole_dy
    down_share = lax.psum_scatter(
        lax.dot_general(
            columns, mixed_hidden, over_rows, preferred_element_type=jnp.float32
        ).astype(jnp.bfloat16),
        "expert",
        scatter_dimension=0,
        tiled=True,
    ).astype(jnp.float32)
    grad_gate = base_share[:, :hidden_part].astype(jnp.bfloat16)
    grad_up = base_share[:, hidden_part:].astype(jnp.bfloat16)
    grad_down = down_share.T.astype(jnp.bfloat16)
    partial_tokens = lax.dot_general(
        summed, full_both, over_cols, preferred_element_type=jnp.float32
    )
    token_grad = lax.psum_scatter(
        partial_tokens.astype(jnp.bfloat16), "width", scatter_dimension=1, tiled=True
    ).astype(jnp.float32)
    grad_tokens = (token_grad + token_back).astype(jnp.bfloat16)
    return (grad_tokens, grad_gate, grad_up, grad_down, grad_delta_in, grad_delta_out)


def solution(mesh):
    return jax.shard_map(
        local,
        mesh=mesh,
        in_specs=(
            P("expert", "width"),
            P("expert", "width"),
            P("expert", None),
            P("expert", None),
            P("expert"),
            P("expert", "width"),
            P("expert", "width"),
            P("width", "expert"),
            P("expert", "width", None),
            P("expert", None, None, "width"),
        ),
        out_specs=(
            P("expert", "width"),
            P("expert", "width"),
            P("expert", "width"),
            P("width", "expert"),
            P("expert", "width", None),
            P("expert", None, None, "width"),
        ),
        check_vma=False,
    )
```

profile of v0, /device:TPU:0, one launch (start us, length us, event | category | flops | bytes accessed | tf_op | source)
XLA Modules:
  0.0 932.4 jit_solution(17404453836838803674)
XLA Ops:
  8.0 1.9 maximum_bitcast_fusion
  12.1 10.1 %all_gather.14 = bf16[128,2880]{0,1:T(8,128)(2,1)} all-gather(bf16[128,720]{0,1:T(8,128)(2,1)} %param.11), channel_id=1, replica_groups=mesh['expert'=32,'width'=4] {'width'}, dimensions={1}, use_global_device_ids=true | all-gather | bytes 921600 | tf_op jit(solution)/shard_map/all_gather | solution.py:22
  22.2 10.1 %all_gather.13 = bf16[128,2880]{0,1:T(8,128)(2,1)} all-gather(bf16[128,720]{0,1:T(8,128)(2,1)} %param.10), channel_id=1, replica_groups=mesh['expert'=32,'width'=4] {'width'}, dimensions={1}, use_global_device_ids=true | all-gather | bytes 921600 | tf_op jit(solution)/shard_map/all_gather | solution.py:21
  32.4 65.0 %all-gather.7.cloned.1.call-done = bf16[32,90,720]{2,1,0:T(8,128)(2,1)} async-done(((bf16[1,90,720]{2,1,0:T(8,128)(2,1)}), bf16[32,90,720]{2,1,0:T(8,128)(2,1)}) %all-gather.7.cloned.1.call-update) | async-done | bytes 4147216 | tf_op jit(solution)/shard_map/all_gather | solution.py:31
  97.4 7.5 reshape.121
  104.9 4.3 fusion.47
  109.2 2.5 convolution_convert_fusion.9
  111.7 96.8 %all-gather.5.cloned.1.call-done = bf16[32,90,1440]{2,1,0:T(8,128)(2,1)} async-done(((bf16[1,90,1440]{2,1,0:T(8,128)(2,1)}), bf16[32,90,1440]{2,1,0:T(8,128)(2,1)}) %all-gather.5.cloned.1.call-update) | async-done | bytes 8294416 | tf_op jit(solution)/shard_map/all_gather | solution.py:25
  208.5 11.0 %reshape.119 = bf16[2880,1440]{1,0:T(8,128)(2,1)} reshape(bf16[32,90,1440]{2,1,0:T(8,128)(2,1)} %all-gather.5.cloned.1.call-done) | data formatting | bytes 16588800
  219.6 6.2 fusion.4
  227.0 2.1 pad_maximum_fusion
  229.1 6.2 copy.125
  235.3 7.3 reshape.111
  242.6 4.3 copy.126
  246.9 52.6 %all_to_all.30 = bf16[32,4,5,2880]{3,1,2,0:T(4,128)(2,1)S(1)} all-to-all(bf16[32,4,5,2880]{3,1,2,0:T(4,128)(2,1)S(1)} %copy.126), channel_id=1, replica_groups=mesh['expert'=32,'width'=4] {'expert'}, dimensions={0} | all-to-all | bytes 7372800 | tf_op jit(solution)/shard_map/all_to_all | solution.py:54
  299.4 1.9 copy-done.1
  301.3 2.3 fusion.46
  304.6 1.5 convolution_convert_fusion.10
  306.3 4.1 slice.52
  310.4 2.5 copy_convert_fusion
  312.9 6.5 reshape.117
  319.4 22.2 %all-reduce.7.cloned.1.call-done = bf16[4,160,512]{2,1,0:T(8,128)(2,1)} async-done(((bf16[4,160,512]{2,1,0:T(8,128)(2,1)}), bf16[4,160,512]{2,1,0:T(8,128)(2,1)}) %all-reduce.7.cloned.1.call-update) | async-done | bytes 655376 | tf_op jit(solution)/shard_map/psum | solution.py:65
  341.6 6.1 copy_add_fusion
  347.7 2.2 fusion.45
  352.4 2.1 fusion.20
  354.5 2.9 maximum_convert_fusion
  357.7 4.2 copy.135
  361.9 2.5 copy.134
  364.5 3.3 copy.136
  367.8 6.2 convert_element_type.132
  374.0 4.1 fusion.16
  378.1 18.8 %all-reduce.9.cloned.1.call-done = bf16[4,160,512]{2,1,0:T(8,128)(2,1)} async-done(((bf16[4,160,512]{2,1,0:T(8,128)(2,1)}), bf16[4,160,512]{2,1,0:T(8,128)(2,1)}) %all-reduce.9.cloned.1.call-update) | async-done | bytes 655376 | tf_op jit(solution)/shard_map/psum | solution.py:85
  396.9 2.1 convolution_convert_fusion.8
  399.0 1.7 copy.133
  400.7 13.1 %concatenate.19 = bf16[4,32,5,2880]{3,0,2,1:T(4,128)(2,1)} concatenate(bf16[4,32,5,720]{3,0,2,1:T(4,128)(2,1)} %bitcast.111, bf16[4,32,5,720]{3,0,2,1:T(4,128)(2,1)} %fusion.16, bf16[4,32,5,1440]{3,0,2,1:T(4,128)(2,1)} %convert_element_type.132), dimensions={3} | concatenate | bytes 7372800 | tf_op jit(solution)/shard_map/concatenate | solution.py:93
  413.8 57.8 %all_to_all.31 = bf16[4,32,5,2880]{3,0,2,1:T(4,128)(2,1)S(1)} all-to-all(bf16[4,32,5,2880]{3,0,2,1:T(4,128)(2,1)} %concatenate.19), channel_id=1, replica_groups=mesh['expert'=32,'width'=4] {'expert'}, dimensions={1} | all-to-all | bytes 7372800 | tf_op jit(solution)/shard_map/all_to_all | solution.py:97
  471.6 3.5 copy.137
  475.0 8.0 reshape.115
  483.0 3.3 convolution_convert_fusion.5
  487.0 6.9 convolution_convert_fusion.3
  494.0 2.9 convolution_convert_fusion.11
  497.0 4.5 fusion.3
  501.5 5.6 fusion
  509.0 6.1 convolution_convert_fusion.4
  515.2 2.6 convolution_convert_fusion.7
  517.8 2.4 fusion.23
  520.2 400.1 %all-reduce.11.cloned.1.call-done = (bf16[2880,1440]{0,1:T(8,128)(2,1)}, bf16[2880,720]{0,1:T(8,128)(2,1)}) async-done(((bf16[2880,1440]{0,1:T(8,128)(2,1)}, bf16[2880,720]{0,1:T(8,128)(2,1)}), (bf16[2880,1440]{0,1:T(8,128)(2,1)}, bf16[2880,720]{0,1:T(8,128)(2,1)})) %all-reduce.11.cloned.1.call-update) | async-done | bytes 12441616
  920.3 1.3 fusion.44
  (79 shorter events, 13.6 us)
Async XLA Ops:
  7.2 297.4 %copy-start = (bf16[4,720,512]{2,1,0:T(8,128)(2,1)S(1)}, bf16[4,720,512]{2,1,0:T(8,128)(2,1)}, u32[]{:S(2)}) copy-start(bf16[4,720,512]{2,1,0:T(8,128)(2,1)} %param.18) | copy-start | bytes 8847364
  7.2 4.6 copy-start.15
  7.2 4.6 copy-start.16
  7.2 90.2 %all-gather.7.cloned.1.call-start = ((), (), s32[]{:S(2)}) async-start(), calls=%async_computation.7 | async-start | bytes 4866048 | tf_op jit(solution)/shard_map/all_gather | solution.py:31
  7.9 200.6 %all-gather.5.cloned.1.call-start = ((), (), s32[]{:S(2)}) async-start(), calls=%async_computation.6 | async-start | bytes 9732096 | tf_op jit(solution)/shard_map/all_gather | solution.py:25
  9.9 331.7 %all-reduce.7.cloned.1.call-start = ((), (), s32[]{:S(2)}) async-start(), calls=%async_computation.3 | async-start | bytes 1310720 | tf_op jit(solution)/shard_map/psum | solution.py:65
  219.6 6.3 copy-start.14
  225.8 1.2 copy-start.9
  299.4 1.9 copy-start.1
  303.6 1.0 copy-start.4
  303.6 2.6 copy-start.17
  306.2 90.7 %all-reduce.9.cloned.1.call-start = ((), (), s32[]{:S(2)}) async-start(), calls=%async_computation.4 | async-start | bytes 1310720 | tf_op jit(solution)/shard_map/psum | solution.py:85
  341.6 10.8 %slice-start = ((s8[5898240]{0:T(1024)(128)(4,1)}), s8[4194304]{0:T(1024)(128)(4,1)S(1)}, s32[]{:S(2)}) async-start(s8[5898240]{0:T(1024)(128)(4,1)} %bitcast.109), calls=%async_computation.9 | async-start | bytes 8388608
  347.7 2.2 copy-start.8
  347.7 4.7 slice-start.1
  351.1 1.0 copy-start.6
  351.1 1.2 copy-start.7
  357.4 160.3 %reduce-scatter.4.cloned.1.call-start = ((), (), s32[]{:S(2)}) async-start(), calls=%async_computation.5 | async-start | bytes 921600 | tf_op jit(solution)/shard_map/reduce_scatter | solution.py:134
  357.7 4.3 copy-start.3
  361.9 2.5 copy-start.2
  486.3 0.7 copy-start.12
  493.9 426.3 %all-reduce.11.cloned.1.call-start = ((), (), s32[]{:S(2)}) async-start(), calls=%async_computation.8 | async-start | bytes 25436160
  496.9 4.5 copy-start.10
  496.9 4.5 copy-start.13
  507.1 0.7 copy-start.18
  509.0 6.2 copy-start.5
  509.0 6.2 copy-start.11
Sparse Core Ops, SparseCore 0:
  11.1 86.2 all-gather.6
  100.5 108.0 all-gather.4
  306.3 35.2 all-reduce.6
  357.5 39.2 all-reduce.8
  494.1 14.8 reduce-scatter.3
  511.4 408.7 all-reduce.10
where the time goes:
time: 943 us; the launch traced here: 932 us
  waiting for transfers between devices  604 us (64%)
  blocking collectives  131 us (14%)
  local copies, waits for them, and re-layouts  106 us (11%)
  matrix products  60.4 us (6%)
  other arithmetic  15.6 us (2%)
  between operations  15.5 us (2%)
    unnamed x7, waiting for transfers between devices  401 us
    all_gather x1, waiting for transfers between devices, local(): full_both = lax.all_gather(weight_both, 'expert', axis=0, tiled=True)  96.8 us
    all_gather x1, waiting for transfers between devices, local(): lax.all_gather(w_down, 'expert', axis=1, tiled=True)  65 us
    all_to_all x1, blocking collectives, local(): lax.all_to_all(returning, 'expert', split_axis=1, concat_axis=0, tiled=True)  57.8 us
    all_to_all x1, blocking collectives, local(): lax.all_to_all(outgoing, 'expert', split_axis=0, concat_axis=2, tiled=True)  52.6 us
    unnamed x50, local copies, waits for them, and re-layouts  28.1 us
    psum x1, waiting for transfers between devices, local(): lax.psum(partial_low.astype(jnp.bfloat16), 'width').astype(jnp.float32)  22.2 us
  transfers between devices with their start and end apart: 6, of which 5 were waited for; matrix products, arithmetic and copies ran while one was open for 8% of the time, Pallas kernels for 0%

commit v1 on v0

v1 whole, which is shorter than its diff:
```python
import jax
import jax.numpy as jnp
from jax import lax
from jax.sharding import Mesh, PartitionSpec as P

BF = jnp.bfloat16
F32 = jnp.float32
EXPERT = ("yh", "z", "x")
PLANE = ("z", "x")
WIDTH = ("yl", "c")
COLUMN = ("yh", "yl", "c")
CAP = 5
HALF = 384


def dot(a, b, dims):
    return lax.dot_general(a, b, (dims, ((), ())), preferred_element_type=F32)


def bdot(a, b, dims):
    return lax.dot_general(a, b, (dims, ((0,), (0,))), preferred_element_type=F32)


def targets_of(routes, experts):
    flat = routes.reshape(-1, 1)
    pairs = flat.shape[0]
    onehot = (flat == lax.broadcasted_iota(jnp.int32, (pairs, experts), 1)).astype(BF)
    earlier = lax.broadcasted_iota(jnp.int32, (pairs, pairs), 0) > lax.broadcasted_iota(
        jnp.int32, (pairs, pairs), 1
    )
    before = dot(earlier.astype(BF), onehot, ((1,), (0,)))
    place = jnp.sum(before * onehot.astype(F32), axis=1).astype(jnp.int32)
    return (flat[:, 0] * CAP + place).reshape(routes.shape)


def width_sum(partial, mask):
    parts = lax.all_to_all(partial.astype(BF), WIDTH, 0, 0)
    total = jnp.sum(parts.astype(F32), axis=0)
    mine = (total * mask).astype(BF)
    return lax.all_gather(mine, WIDTH)


def pad_cols(a):
    return jnp.pad(a, ((0, 0),) * (a.ndim - 1) + ((0, 2 * HALF - a.shape[-1]),))


def local(tokens, grad_out, routes, gates, ranks, w_gate, w_up, w_down, delta_in, delta_out):
    yh = lax.axis_index("yh")
    wi = lax.axis_index("yl") * 2 + lax.axis_index("c")
    rows, part = tokens.shape
    local_e, _, rank_max = delta_in.shape
    n_exp = 32
    experts = n_exp * local_e
    per_dev = local_e * CAP
    slots = experts * CAP
    er = n_exp * CAP
    wr = w_gate.shape[0]

    w3 = jnp.stack([pad_cols(w_gate), pad_cols(w_up), pad_cols(w_down.T)], axis=1)
    keep = lax.dynamic_slice_in_dim(w3, yh * HALF, HALF, 2).reshape(wr, 3 * HALF)
    give = lax.dynamic_slice_in_dim(w3, (1 - yh) * HALF, HALF, 2).reshape(wr, 3 * HALF)
    got = lax.ppermute(give, "yh", [(0, 1), (1, 0)])
    both = jnp.where(yh == 0, jnp.stack([keep, got]), jnp.stack([got, keep]))
    full = lax.all_gather(both, PLANE)
    full = full.transpose(1, 0, 2, 3).reshape(4, part, 3 * HALF)

    xy = lax.all_gather(jnp.stack([tokens, grad_out]), COLUMN)
    xy = xy.reshape(2, 4, 2, rows, part)
    xs = [jnp.concatenate([xy[0, w, 0], xy[1, w, 0]], axis=0) for w in range(4)]
    ys = [jnp.concatenate([xy[0, w, 1], xy[1, w, 1]], axis=0) for w in range(4)]

    target = targets_of(routes, experts)
    slot_ids = lax.broadcasted_iota(jnp.int32, (slots, rows), 0)
    picker = sum((target[None, :, k] == slot_ids).astype(F32) for k in range(4)).astype(BF)
    target2 = lax.all_gather(target, "yh")
    gates2 = lax.all_gather(gates, "yh")
    block_of = lax.broadcasted_iota(jnp.int32, (2, rows, 4), 0)
    place2 = (target2 // per_dev) * (2 * per_dev) + block_of * per_dev + target2 % per_dev
    place2 = place2.reshape(2 * rows, 4)
    gates2 = gates2.reshape(2 * rows, 4)
    ids2 = lax.broadcasted_iota(jnp.int32, (2 * slots, 2 * rows), 0)
    hits = [place2[None, :, k] == ids2 for k in range(4)]
    picker2 = sum(h.astype(F32) for h in hits).astype(BF)
    gate_slot = jnp.sum(
        sum(jnp.where(h, gates2[None, :, k], 0.0) for k, h in enumerate(hits)), axis=1, keepdims=True
    )

    r_exp = lax.broadcasted_iota(jnp.int32, (slots, slots), 0)
    s_in = lax.broadcasted_iota(jnp.int32, (slots, slots), 1)
    e_r, zx_r, b_r, p_r = r_exp // er, (r_exp % er) // (2 * CAP), (r_exp % (2 * CAP)) // CAP, r_exp % CAP
    perm_x = (s_in == (b_r * 16 + zx_r) * per_dev + e_r * CAP + p_r).astype(BF)
    perm_p = (s_in == (zx_r * 2 + b_r) * per_dev + e_r * CAP + p_r).astype(BF)

    out_x = dot(picker, tokens, ((1,), (0,))).astype(BF).reshape(n_exp, per_dev, part)
    in_x = lax.all_to_all(out_x, EXPERT, 0, 0).reshape(slots, part)
    rows_x = dot(perm_x, in_x, ((1,), (0,))).astype(BF).reshape(local_e, er, part)
    rank_ids = lax.broadcasted_iota(jnp.int32, (1, rank_max), 1)
    mask = (rank_ids < ranks[wi]).astype(F32)
    low = width_sum(bdot(rows_x, delta_in, ((2,), (1,))), mask)
    halves = []
    for h in range(2):
        cols = []
        for c in range(2):
            d = bdot(low, delta_out[:, :, c, h * HALF : min(part, (h + 1) * HALF)], ((2,), (1,)))
            d = d.astype(BF)
            if h == 1:
                d = jnp.pad(d, ((0, 0), (0, 0), (0, 2 * HALF - part)))
            cols.append(d)
        cols = jnp.concatenate(cols, axis=2).reshape(slots, 2 * HALF)
        halves.append(dot(perm_p, cols, ((0,), (0,))).astype(BF).reshape(16, 2 * per_dev, 2 * HALF))
    back_pre = lax.all_to_all(jnp.concatenate(halves, axis=0), EXPERT, 0, 0)
    back_pre = back_pre.reshape(2 * slots, 2 * HALF)

    base = sum(dot(xs[w], full[w, :, : 2 * HALF], ((1,), (0,))) for w in range(4)).astype(BF)
    down = sum(dot(ys[w], full[w, :, 2 * HALF :], ((1,), (0,))) for w in range(4)).astype(BF)
    pre = dot(picker2, base, ((1,), (0,))) + back_pre.astype(F32)
    pair_down = (gate_slot * dot(picker2, down, ((1,), (0,)))).astype(BF).astype(F32)
    act, up = pre[:, :HALF], pre[:, HALF:]
    sig = jax.nn.sigmoid(act)
    swish = act * sig
    weighted = (gate_slot * (swish * up)).astype(BF)
    grad_act = pair_down * up * sig * (1.0 + act * (1.0 - sig))
    grad_up_ = pair_down * swish
    pair_grad = jnp.concatenate([grad_act, grad_up_], axis=1).astype(BF)
    mixed = dot(picker2, weighted, ((0,), (0,))).astype(BF)
    summed = dot(picker2, pair_grad, ((0,), (0,))).astype(BF)

    dw = jnp.stack(
        [
            jnp.concatenate(
                [dot(xs[w], summed, ((0,), (0,))), dot(ys[w], mixed, ((0,), (0,)))], axis=1
            ).astype(BF)
            for w in range(4)
        ]
    )
    dw = dw.reshape(2, 16, wr, 3 * HALF).transpose(1, 0, 2, 3).reshape(16, 2 * wr, 3 * HALF)
    dw = lax.psum_scatter(dw, PLANE).reshape(2, wr, 3 * HALF)
    mine = lax.dynamic_index_in_dim(dw, yh, 0, keepdims=False)
    other = lax.dynamic_index_in_dim(dw, 1 - yh, 0, keepdims=False)
    other = lax.ppermute(other, "yh", [(0, 1), (1, 0)])
    lo = jnp.where(yh == 0, mine, other)
    hi = jnp.where(yh == 0, other, mine)
    rest = part - HALF
    grads = [
        jnp.concatenate([lo[:, i * HALF : (i + 1) * HALF], hi[:, i * HALF : i * HALF + rest]], axis=1)
        for i in range(3)
    ]

    in_p = lax.all_to_all(pair_grad.reshape(n_exp, 2 * per_dev, 2 * HALF), EXPERT, 0, 0)
    in_p = in_p.reshape(2, slots, 2 * HALF)
    pg = [dot(perm_p, in_p[h], ((1,), (0,))).astype(BF) for h in range(2)]
    pg = jnp.stack(
        [
            jnp.concatenate([pg[0][:, c * HALF : (c + 1) * HALF], pg[1][:, c * HALF : c * HALF + rest]], axis=1)
            for c in range(2)
        ],
        axis=1,
    ).reshape(local_e, er, 2, part)
    low_back = lax.dot_general(
        pg, delta_out, (((2, 3), (2, 3)), ((0,), (0,))), preferred_element_type=F32
    )
    low_grad = width_sum(low_back, mask)
    grad_delta_out = lax.dot_general(
        low, pg, (((1,), (1,)), ((0,), (0,))), preferred_element_type=F32
    ).astype(BF)
    grad_delta_in = bdot(rows_x, low_grad, ((1,), (1,))).astype(BF)
    back = bdot(low_grad, delta_in, ((2,), (2,))).astype(BF).reshape(slots, part)
    back = dot(perm_x, back, ((0,), (0,))).astype(BF).reshape(n_exp, per_dev, part)
    back = lax.all_to_all(back, EXPERT, 0, 0).reshape(slots, part)
    token_back = dot(picker, back, ((0,), (0,)))

    dx = jnp.stack([dot(summed, full[w, :, : 2 * HALF], ((1,), (1,))) for w in range(4)]).astype(BF)
    dx = dx.reshape(4, 2, rows, part).transpose(1, 0, 2, 3).reshape(8, rows, part)
    dx = lax.psum_scatter(dx, COLUMN).astype(F32)
    grad_tokens = (dx + token_back).astype(BF)
    return (grad_tokens, grads[0], grads[1], grads[2].T, grad_delta_in, grad_delta_out)


def solution(mesh):
    fine = Mesh(mesh.devices.reshape(2, 4, 4, 2, 2), ("yh", "z", "x", "yl", "c"))
    return jax.shard_map(
        local,
        mesh=fine,
        in_specs=(
            P(EXPERT, WIDTH),
            P(EXPERT, WIDTH),
            P(EXPERT, None),
            P(EXPERT, None),
            P(EXPERT),
            P(EXPERT, WIDTH),
            P(EXPERT, WIDTH),
            P(WIDTH, EXPERT),
            P(EXPERT, WIDTH, None),
            P(EXPERT, None, None, WIDTH),
        ),
        out_specs=(
            P(EXPERT, WIDTH),
            P(EXPERT, WIDTH),
            P(EXPERT, WIDTH),
            P(WIDTH, EXPERT),
            P(EXPERT, WIDTH, None),
            P(EXPERT, None, None, WIDTH),
        ),
        check_vma=False,
    )
```

time: 943 us -> 376 us (0.40)
  waiting for transfers between devices: 604 us -> 99.4 us
  blocking collectives: 131 us -> 31 us
  starting transfers between devices: 0.46 us -> 45.9 us
  local copies, waits for them, and re-layouts: 106 us -> 66.4 us
  matrix products: 60.4 us -> 92.4 us
    unnamed x7 -> x5, waiting for transfers between devices: 401 us -> 0.07 us
    all_gather x2, waiting for transfers between devices: 162 us -> 0.04 us  [the longest x1 0.02 us: local(): xy = lax.all_gather(jnp.stack([tokens, grad_out]), COLUMN)]
    all_to_all x2 -> x0, blocking collectives: 110 us -> none  [the longest x1 57.8 us: local(): lax.all_to_all(returning, 'expert', split_axis=1, concat_axis=0, tiled=True)]
    all_to_all x0 -> x6, waiting for transfers between devices: none -> 66.6 us  [the longest x1 29.5 us: local(): lax.all_to_all(pair_grad.reshape(n_exp, 2 * per_dev, 2 * HALF), EXPERT, 0...]
    psum x2 -> x0, waiting for transfers between devices: 41 us -> none  [the longest x1 22.2 us: local(): lax.psum(partial_low.astype(jnp.bfloat16), 'width').astype(jnp.float32)]
    all_to_all x0 -> x6, starting transfers between devices: none -> 40.9 us  [the longest x1 11 us: local(): in_x = lax.all_to_all(out_x, EXPERT, 0, 0).reshape(slots, part)]
    dot_general x16 -> x40, matrix products: 60.4 us -> 92.4 us  [the longest x31 69.5 us: dot(): return lax.dot_general(a, b, (dims, ((), ())), preferred_element_type=F32)]
    reduce_scatter x1, waiting for transfers between devices: 0.01 us -> 27.3 us  [local(): dx = lax.psum_scatter(dx, COLUMN).astype(F32)]
  transfers between devices with their start and end apart: 6 -> 12, of which waited for: 5 -> 7; matrix products, arithmetic and copies ran while one was open for 8% -> 33% of each run, Pallas kernels for 0% -> 0%
where the time goes in v1:
time: 376 us; the launch traced here: 369 us
  waiting for transfers between devices  99.4 us (26%)
  matrix products  92.4 us (25%)
  local copies, waits for them, and re-layouts  66.4 us (18%)
  starting transfers between devices  45.9 us (12%)
  blocking collectives  31 us (8%)
  other arithmetic  18.6 us (5%)
  between operations  15.2 us (4%)
    dot_general x31, matrix products, dot(): return lax.dot_general(a, b, (dims, ((), ())), preferred_element_type=F32)  69.5 us
    all_to_all x1, waiting for transfers between devices, local(): lax.all_to_all(pair_grad.reshape(n_exp, 2 * per_dev, 2 * HALF), EXPERT, 0...  29.5 us
    reduce_scatter x1, waiting for transfers between devices, local(): dx = lax.psum_scatter(dx, COLUMN).astype(F32)  27.3 us
    all_to_all x1, waiting for transfers between devices, local(): in_x = lax.all_to_all(out_x, EXPERT, 0, 0).reshape(slots, part)  19.4 us
    all_gather x2, blocking collectives, width_sum(): return lax.all_gather(mine, WIDTH)  15.5 us
    dot_general x7, matrix products, bdot(): lax.dot_general(a, b, (dims, ((0,), (0,))), preferred_element_type=F32)  14.7 us
    reshape x2, local copies, waits for them, and re-layouts, local(): dw.reshape(2, 16, wr, 3 * HALF).transpose(1, 0, 2, 3)  13 us
    all_to_all x1, waiting for transfers between devices, local(): back = lax.all_to_all(back, EXPERT, 0, 0).reshape(slots, part)  12.4 us
  transfers between devices with their start and end apart: 12, of which 7 were waited for; matrix products, arithmetic and copies ran while one was open for 33% of the time, Pallas kernels for 0%

profile of v1, /device:TPU:0, one launch (start us, length us, event | category | flops | bytes accessed | tf_op | source)
XLA Modules:
  0.0 368.9 jit_solution(495467272413840103)
XLA Ops:
  12.3 3.3 collective-permute-start
  16.0 5.4 %collective-permute-done = bf16[90,1152]{1,0:T(8,128)(2,1)} collective-permute-done((bf16[90,1152]{1,0:T(8,128)(2,1)}, bf16[90,1152]{1,0:T(8,128)(2,1)}, u32[]{:S(2)}, u32[]{:S(2)}) %collective-permute-start) | collective-permute-done | bytes 207392 | tf_op jit(solution)/shard_map/ppermute | solution.py:62
  26.4 2.2 copy.136
  30.8 11.0 %all-to-all-start = ((bf16[32,20,720]{2,1,0:T(8,128)(2,1)}), bf16[32,20,720]{2,1,0:T(8,128)(2,1)}, u32[]{:S(2)}, u32[]{:S(2)}) async-start(bf16[32,20,720]{2,1,0:T(8,128)(2,1)} %reshape.398), calls=%async_computation | async-start | bytes 2359296 | tf_op jit(solution)/shard_map/all_to_all | solution.py:95
  41.9 19.4 %all-to-all-done = bf16[32,20,720]{2,1,0:T(8,128)(2,1)} async-done(((bf16[32,20,720]{2,1,0:T(8,128)(2,1)}), bf16[32,20,720]{2,1,0:T(8,128)(2,1)}, u32[]{:S(2)}, u32[]{:S(2)}) %all-to-all-start) | async-done | bytes 921632 | tf_op jit(solution)/shard_map/all_to_all | solution.py:95
  61.4 2.3 reshape.399
  63.7 5.9 %convolution_convert_fusion.13 = bf16[640,720]{0,1:T(8,128)(2,1)} fusion(bf16[640,720]{1,0:T(8,128)(2,1)} %reshape.399, s32[640]{0:T(1024)S(1)} %get-tuple-element.52, s32[640]{0:T(1024)S(1)} %get-tuple-element.58, s32[640]{0:T(1024)S(1)} %get-tuple-element.53, s32[640]{0:T(1024)S(1)} %get-tuple-element.59, pred[640]{0:T(1024)(128)(4,1)S(1)} %get-tuple-element.62, ...), kind=kOutput, calls=%fused_computation.60 | convolution fusion | flops 601344000 | bytes 1866240 | tf_op jit(solution)/shard_map/dot_general | solution.py:17
  69.5 2.3 copy.137
  71.8 2.7 convolution_convert_fusion.14
  74.6 4.2 %all-to-all-start.1 = ((bf16[4,160,512]{2,1,0:T(8,128)(2,1)}), bf16[4,160,512]{2,1,0:T(8,128)(2,1)}, u32[]{:S(2)}, u32[]{:S(2)}) async-start(bf16[4,160,512]{2,1,0:T(8,128)(2,1)} %convolution_convert_fusion.14), calls=%async_computation.1 | async-start | bytes 1310720 | tf_op jit(solution)/shard_map/all_to_all | solution.py:37
  79.4 9.7 %all-gather = s32[256,4]{0,1:T(4,128)S(1)} all-gather(s32[128,4]{0,1:T(4,128)S(1)} %multiply_add_fusion), channel_id=2, replica_groups=mesh['yh'=2,'z'=4,'x'=4,'yl'=2,'c'=2] {'yh'}, dimensions={0}, use_global_device_ids=true | all-gather | bytes 6144 | tf_op jit(solution)/shard_map/all_gather | solution.py:75
  89.0 5.8 %all-gather.1 = f32[256,4]{0,1:T(4,128)S(1)} all-gather(f32[128,4]{0,1:T(4,128)S(1)} %copy-done.57), channel_id=3, replica_groups=mesh['yh'=2,'z'=4,'x'=4,'yl'=2,'c'=2] {'yh'}, dimensions={0}, use_global_device_ids=true | all-gather | bytes 6144 | tf_op jit(solution)/shard_map/all_gather | solution.py:76
  96.9 8.0 %all_gather.33 = bf16[4,160,512]{2,1,0:T(8,128)(2,1)S(1)} all-gather(bf16[1,160,512]{2,1,0:T(8,128)(2,1)S(1)} %fusion.85), channel_id=1, replica_groups=mesh['yh'=2,'z'=4,'x'=4,'yl'=2,'c'=2] {'yl','c'}, dimensions={0}, use_global_device_ids=true | all-gather | bytes 819200 | tf_op jit(solution)/shard_map/all_gather | solution.py:40
  104.8 2.2 fusion.37
  119.0 7.2 %all-to-all-start.2 = ((bf16[32,40,768]{2,1,0:T(8,128)(2,1)}), bf16[32,40,768]{2,1,0:T(8,128)(2,1)}, u32[]{:S(2)}, u32[]{:S(2)}) async-start(bf16[32,40,768]{2,1,0:T(8,128)(2,1)} %pad_maximum_fusion), calls=%async_computation.2 | async-start | bytes 3932160 | tf_op jit(solution)/shard_map/all_to_all | solution.py:111
  126.9 3.3 slice_bitcast_fusion.10
  130.2 6.8 %copy.135 = bf16[2,16,90,1152]{3,2,1,0:T(8,128)(2,1)} copy(bf16[2,16,90,1152]{3,0,2,1:T(2,128)(2,1)} %bitcast.266) | data formatting | bytes 13271040 | tf_op jit(solution)/shard_map/transpose | solution.py:65
  137.0 8.9 %reshape.397 = bf16[4,720,1152]{2,1,0:T(8,128)(2,1)} reshape(bf16[2,16,90,1152]{3,2,1,0:T(8,128)(2,1)} %copy.135) | data formatting | bytes 13271040 | tf_op jit(solution)/shard_map/reshape | solution.py:65
  145.9 2.4 fusion.83
  152.0 2.7 convolution_add_fusion.2
  154.8 5.6 %convolution_add_fusion = f32[1280,768]{1,0:T(8,128)} fusion(bf16[1280,768]{1,0:T(8,128)(2,1)} %bitcast.104, f32[256,768]{1,0:T(8,128)} %convolution_add_fusion.2, bf16[4,720,1152]{2,1,0:T(8,128)(2,1)} %reshape.397, s32[256]{0:T(256)S(1)} %bitcast.296, s32[256]{0:T(256)S(1)} %bitcast.301, s32[256]{0:T(256)S(1)} %bitcast.306, s32[256]{0:T(256)S(1)} %bitcast.291, ...), kind=kOutput, calls=%fused_computation.1 | convolution fusion | flops 793460736 | bytes 8163328 | tf_op jit(solution)/shard_map/dot_general | solution.py:17
  160.4 3.6 convolution_convert_fusion.23
  169.2 2.2 convolution_add_fusion.5
  172.6 5.6 %multiply_convert_fusion.2 = (bf16[1280,384]{1,0:T(8,128)(2,1)}, bf16[1280,384]{1,0:T(8,128)(2,1)}) fusion(f32[1280,768]{1,0:T(8,128)} %convolution_add_fusion, f32[256,384]{1,0:T(8,128)} %convolution_add_fusion.5, bf16[4,720,1152]{2,1,0:T(8,128)(2,1)} %reshape.397, bf16[128,720]{0,1:T(8,128)(2,1)S(1)} %copy-done.26, bf16[128,720]{0,1:T(8,128)(2,1)S(1)} %copy-done.27, ...), kind=kOutput, calls=%fused_computation.28 | convolution fusion | flops 405946368 | bytes 7222272 | tf_op jit(solution)/shard_map/dot_general | solution.py:17
  178.2 2.5 fusion.47
  183.8 3.6 maximum_maximum_fusion
  187.3 8.9 %reshape.410 = bf16[2,16,90,1152]{3,2,1,0:T(8,128)(2,1)} reshape(bf16[4,720,1152]{2,1,0:T(8,128)(2,1)} %maximum_maximum_fusion) | data formatting | bytes 13271040 | tf_op jit(solution)/shard_map/reshape | solution.py:136
  196.3 5.3 %copy.146 = bf16[16,2,90,1152]{3,0,2,1:T(8,128)(2,1)S(1)} copy(bf16[16,2,90,1152]{3,2,0,1:T(8,128)(2,1)} %bitcast.262) | data formatting | bytes 13271040 | tf_op jit(solution)/shard_map/transpose | solution.py:136
  201.5 4.1 %copy.147 = bf16[16,180,1152]{2,1,0:T(8,128)(2,1)} copy(bf16[16,180,1152]{2,0,1:T(8,128)(2,1)S(1)} %bitcast.263) | data formatting | bytes 13271040 | tf_op jit(solution)/shard_map/reshape | solution.py:136
  205.6 2.9 pad_maximum_fusion.1
  208.6 9.8 %all-to-all-start.3 = ((bf16[32,40,768]{2,1,0:T(8,128)(2,1)}), bf16[32,40,768]{2,1,0:T(8,128)(2,1)}, u32[]{:S(2)}, u32[]{:S(2)}) async-start(bf16[32,40,768]{2,1,0:T(8,128)(2,1)} %pad_maximum_fusion.1), calls=%async_computation.4 | async-start | bytes 3932160 | tf_op jit(solution)/shard_map/all_to_all | solution.py:149
  218.3 2.5 fusion.57
  220.8 2.5 fusion.56
  223.4 29.5 %all-to-all-done.3 = bf16[32,40,768]{2,1,0:T(8,128)(2,1)} async-done(((bf16[32,40,768]{2,1,0:T(8,128)(2,1)}), bf16[32,40,768]{2,1,0:T(8,128)(2,1)}, u32[]{:S(2)}, u32[]{:S(2)}) %all-to-all-start.3) | async-done | bytes 1966112 | tf_op jit(solution)/shard_map/all_to_all | solution.py:149
  254.6 3.8 %convolution_convert_fusion.7 = bf16[640,768]{1,0:T(8,128)(2,1)S(1)} fusion(bf16[640,768]{1,0:T(8,128)(2,1)S(1)} %bitcast.285, s32[640]{0:T(1024)S(1)} %copy-done.46, s32[640]{0:T(1024)S(1)} %get-tuple-element.58, s32[640]{0:T(1024)S(1)} %copy-done.48, s32[640]{0:T(1024)S(1)} %get-tuple-element.59, pred[640]{0:T(1024)(128)(4,1)S(1)} %copy-done.59, ...), kind=kOutput, calls=%fused_computation.54 | convolution fusion | flops 640696320 | bytes 1989120 | tf_op jit(solution)/shard_map/dot_general | solution.py:17
  258.6 3.8 %convolution_convert_fusion.8 = bf16[640,768]{1,0:T(8,128)(2,1)S(1)} fusion(bf16[640,768]{1,0:T(8,128)(2,1)S(1)} %bitcast.283, s32[640]{0:T(1024)S(1)} %copy-done.46, s32[640]{0:T(1024)S(1)} %get-tuple-element.58, s32[640]{0:T(1024)S(1)} %copy-done.48, s32[640]{0:T(1024)S(1)} %get-tuple-element.59, pred[640]{0:T(1024)(128)(4,1)S(1)} %copy-done.59, ...), kind=kOutput, calls=%fused_computation.55 | convolution fusion | flops 640696320 | bytes 1989120 | tf_op jit(solution)/shard_map/dot_general | solution.py:17
  266.0 4.2 %all-to-all-start.4 = ((bf16[4,160,512]{2,1,0:T(8,128)(2,1)}), bf16[4,160,512]{2,1,0:T(8,128)(2,1)}, u32[]{:S(2)}, u32[]{:S(2)}) async-start(bf16[4,160,512]{2,1,0:T(8,128)(2,1)} %fusion.33), calls=%async_computation.5 | async-start | bytes 1310720 | tf_op jit(solution)/shard_map/all_to_all | solution.py:37
  275.4 5.1 %all-to-all-done.4 = bf16[4,160,512]{2,1,0:T(8,128)(2,1)} async-done(((bf16[4,160,512]{2,1,0:T(8,128)(2,1)}), bf16[4,160,512]{2,1,0:T(8,128)(2,1)}, u32[]{:S(2)}, u32[]{:S(2)}) %all-to-all-start.4) | async-done | bytes 655392 | tf_op jit(solution)/shard_map/all_to_all | solution.py:37
  281.8 7.5 %all_gather.34 = bf16[4,160,512]{2,1,0:T(8,128)(2,1)S(1)} all-gather(bf16[1,160,512]{2,1,0:T(8,128)(2,1)S(1)} %fusion.84), channel_id=1, replica_groups=mesh['yh'=2,'z'=4,'x'=4,'yl'=2,'c'=2] {'yl','c'}, dimensions={0}, use_global_device_ids=true | all-gather | bytes 819200 | tf_op jit(solution)/shard_map/all_gather | solution.py:40
  290.4 2.8 convolution_convert_fusion.12
  293.2 2.4 copy.145
  297.7 4.7 %all-to-all-start.5 = ((bf16[32,20,720]{2,1,0:T(8,128)(2,1)}), bf16[32,20,720]{2,1,0:T(8,128)(2,1)}, u32[]{:S(2)}, u32[]{:S(2)}) async-start(bf16[32,20,720]{2,1,0:T(8,128)(2,1)} %reshape.408), calls=%async_computation.6 | async-start | bytes 2359296 | tf_op jit(solution)/shard_map/all_to_all | solution.py:169
  302.4 6.2 %convolution_convert_fusion = bf16[4,512,2,720]{1,3,2,0:T(8,128)(2,1)} fusion(bf16[4,160,1,720]{3,1,2,0:T(8,128)(2,1)} %bitcast.275, bf16[4,160,1,720]{3,1,2,0:T(8,128)(2,1)} %bitcast.273, bf16[4,160,512]{2,1,0:T(8,128)(2,1)} %copy-done.6), kind=kOutput, calls=%fused_computation.2 | convolution fusion | flops 950353920 | bytes 8396800 | tf_op jit(solution)/shard_map/dot_general | solution.py:163
  308.6 2.6 convolution_convert_fusion.1
  311.2 12.4 %all-to-all-done.5 = bf16[32,20,720]{2,1,0:T(8,128)(2,1)} async-done(((bf16[32,20,720]{2,1,0:T(8,128)(2,1)}), bf16[32,20,720]{2,1,0:T(8,128)(2,1)}, u32[]{:S(2)}, u32[]{:S(2)}) %all-to-all-start.5) | async-done | bytes 921632 | tf_op jit(solution)/shard_map/all_to_all | solution.py:169
  323.6 2.3 reshape.409
  329.3 27.3 %reduce-scatter.5.cloned.1.call-done = bf16[1,128,720]{1,2,0:T(8,128)(2,1)} async-done(((bf16[8,128,720]{1,2,0:T(8,128)(2,1)}), bf16[1,128,720]{1,2,0:T(8,128)(2,1)}) %reduce-scatter.5.cloned.1.call-update) | async-done | bytes 184336 | tf_op jit(solution)/shard_map/reduce_scatter | solution.py:174
  356.6 2.4 fusion.59
  (234 shorter events, 62.2 us)
Async XLA Ops:
  7.2 64.7 %copy-start = (bf16[4,720,512]{2,1,0:T(8,128)(2,1)S(1)}, bf16[4,720,512]{2,1,0:T(8,128)(2,1)}, u32[]{:S(2)}) copy-start(bf16[4,720,512]{2,1,0:T(8,128)(2,1)} %param.18) | copy-start | bytes 8847364
  7.2 119.7 %all-gather.8.cloned.1.call-start = ((), (), s32[]{:S(2)}) async-start(), calls=%async_computation.10 | async-start | bytes 3317760 | tf_op jit(solution)/shard_map/all_gather | solution.py:67
  9.2 121.0 %all-gather.6.cloned.1.call-start = ((), (), s32[]{:S(2)}) async-start(), calls=%async_computation.8 | async-start | bytes 7050240 | tf_op jit(solution)/shard_map/all_gather | solution.py:64
  12.3 11.3 %copy-start.36 = (s32[128,4]{0,1:T(4,128)S(1)}, s32[128,4]{0,1:T(4,128)}, u32[]{:S(2)}) copy-start(s32[128,4]{0,1:T(4,128)} %param.12) | copy-start | bytes 6148
  12.3 9.0 %collective-permute-start = (bf16[90,1152]{1,0:T(8,128)(2,1)}, bf16[90,1152]{1,0:T(8,128)(2,1)}, u32[]{:S(2)}, u32[]{:S(2)}) collective-permute-start(bf16[90,1152]{1,0:T(8,128)(2,1)} %bitcast.118), channel_id=1, source_target_pairs={{0,64},{64,0},{1,65},{65,1},{2,66},{66,2},{3,67},{67,3},{4,68},{68... | collective-permute-start | bytes 622088 | tf_op jit(solution)/shard_map/ppermute | solution.py:62
  15.9 9.0 %copy-start.21 = (bf16[128,720]{0,1:T(8,128)(2,1)S(1)}, bf16[128,720]{0,1:T(8,128)(2,1)}, u32[]{:S(2)}) copy-start(bf16[128,720]{0,1:T(8,128)(2,1)} %param.10) | copy-start | bytes 552964
  30.8 30.6 %all-to-all-start = ((bf16[32,20,720]{2,1,0:T(8,128)(2,1)}), bf16[32,20,720]{2,1,0:T(8,128)(2,1)}, u32[]{:S(2)}, u32[]{:S(2)}) async-start(bf16[32,20,720]{2,1,0:T(8,128)(2,1)} %reshape.398), calls=%async_computation | async-start | bytes 2359296 | tf_op jit(solution)/shard_map/all_to_all | solution.py:95
  41.8 73.6 %copy-start.58 = (pred[640]{0:T(1024)(128)(4,1)}, pred[640]{0:T(1024)(128)(4,1)S(1)}, u32[]{:S(2)}) copy-start(pred[640]{0:T(1024)(128)(4,1)S(1)} %get-tuple-element.62) | copy-start | bytes 1924
  41.8 73.6 %copy-start.60 = (pred[640]{0:T(1024)(128)(4,1)}, pred[640]{0:T(1024)(128)(4,1)S(1)}, u32[]{:S(2)}) copy-start(pred[640]{0:T(1024)(128)(4,1)S(1)} %get-tuple-element.63) | copy-start | bytes 1924
  41.8 73.6 %copy-start.62 = (pred[640]{0:T(1024)(128)(4,1)}, pred[640]{0:T(1024)(128)(4,1)S(1)}, u32[]{:S(2)}) copy-start(pred[640]{0:T(1024)(128)(4,1)S(1)} %get-tuple-element.60) | copy-start | bytes 1924
  41.8 73.6 %copy-start.64 = (pred[640]{0:T(1024)(128)(4,1)}, pred[640]{0:T(1024)(128)(4,1)S(1)}, u32[]{:S(2)}) copy-start(pred[640]{0:T(1024)(128)(4,1)S(1)} %get-tuple-element.61) | copy-start | bytes 1924
  41.8 73.6 %copy-start.37 = (s32[640]{0:T(1024)}, s32[640]{0:T(1024)S(1)}, u32[]{:S(2)}) copy-start(s32[640]{0:T(1024)S(1)} %get-tuple-element.56) | copy-start | bytes 7684
  41.8 73.6 %copy-start.39 = (s32[640]{0:T(1024)}, s32[640]{0:T(1024)S(1)}, u32[]{:S(2)}) copy-start(s32[640]{0:T(1024)S(1)} %get-tuple-element.57) | copy-start | bytes 7684
  41.9 73.6 %copy-start.41 = (s32[640]{0:T(1024)}, s32[640]{0:T(1024)S(1)}, u32[]{:S(2)}) copy-start(s32[640]{0:T(1024)S(1)} %get-tuple-element.54) | copy-start | bytes 7684
  41.9 73.6 %copy-start.43 = (s32[640]{0:T(1024)}, s32[640]{0:T(1024)S(1)}, u32[]{:S(2)}) copy-start(s32[640]{0:T(1024)S(1)} %get-tuple-element.55) | copy-start | bytes 7684
  41.9 73.6 %copy-start.45 = (s32[640]{0:T(1024)}, s32[640]{0:T(1024)S(1)}, u32[]{:S(2)}) copy-start(s32[640]{0:T(1024)S(1)} %get-tuple-element.52) | copy-start | bytes 7684
  41.9 73.6 %copy-start.47 = (s32[640]{0:T(1024)}, s32[640]{0:T(1024)S(1)}, u32[]{:S(2)}) copy-start(s32[640]{0:T(1024)S(1)} %get-tuple-element.53) | copy-start | bytes 7684
  71.8 6.9 %copy-start.66 = (s32[4]{0:T(128)S(1)}, s32[4]{0:T(128)}, u32[]{:S(2)}) copy-start(s32[4]{0:T(128)} %param.14) | copy-start | bytes 52
  71.8 17.2 %copy-start.57 = (f32[128,4]{0,1:T(4,128)S(1)}, f32[128,4]{0,1:T(4,128)}, u32[]{:S(2)}) copy-start(f32[128,4]{0,1:T(4,128)} %param.13) | copy-start | bytes 6148
  74.6 21.0 %all-to-all-start.1 = ((bf16[4,160,512]{2,1,0:T(8,128)(2,1)}), bf16[4,160,512]{2,1,0:T(8,128)(2,1)}, u32[]{:S(2)}, u32[]{:S(2)}) async-start(bf16[4,160,512]{2,1,0:T(8,128)(2,1)} %convolution_convert_fusion.14), calls=%async_computation.1 | async-start | bytes 1310720 | tf_op jit(solution)/shard_map/all_to_all | solution.py:37
  104.8 6.4 %copy-start.6 = (bf16[4,160,512]{2,1,0:T(8,128)(2,1)}, bf16[4,160,512]{2,1,0:T(8,128)(2,1)S(1)}, u32[]{:S(2)}) copy-start(bf16[4,160,512]{2,1,0:T(8,128)(2,1)S(1)} %all_gather.33) | copy-start | bytes 1966084
  119.0 35.8 %all-to-all-start.2 = ((bf16[32,40,768]{2,1,0:T(8,128)(2,1)}), bf16[32,40,768]{2,1,0:T(8,128)(2,1)}, u32[]{:S(2)}, u32[]{:S(2)}) async-start(bf16[32,40,768]{2,1,0:T(8,128)(2,1)} %pad_maximum_fusion), calls=%async_computation.2 | async-start | bytes 3932160 | tf_op jit(solution)/shard_map/all_to_all | solution.py:111
  126.2 199.7 %reduce-scatter.7.cloned.1.call-start = ((), (), s32[]{:S(2)}) async-start(), calls=%async_computation.11 | async-start | bytes 7206912
  130.2 20.0 %copy-start.13 = (bf16[128,720]{0,1:T(8,128)(2,1)}, bf16[128,720]{0,1:T(8,128)(2,1)S(1)}, u32[]{:S(2)}) copy-start(bf16[128,720]{0,1:T(8,128)(2,1)S(1)} %get-tuple-element.12) | copy-start | bytes 552964
  130.2 24.6 %copy-start.11 = (bf16[128,720]{0,1:T(8,128)(2,1)}, bf16[128,720]{0,1:T(8,128)(2,1)S(1)}, u32[]{:S(2)}) copy-start(bf16[128,720]{0,1:T(8,128)(2,1)S(1)} %get-tuple-element.9) | copy-start | bytes 552964
  208.6 44.3 %all-to-all-start.3 = ((bf16[32,40,768]{2,1,0:T(8,128)(2,1)}), bf16[32,40,768]{2,1,0:T(8,128)(2,1)}, u32[]{:S(2)}, u32[]{:S(2)}) async-start(bf16[32,40,768]{2,1,0:T(8,128)(2,1)} %pad_maximum_fusion.1), calls=%async_computation.4 | async-start | bytes 3932160 | tf_op jit(solution)/shard_map/all_to_all | solution.py:149
  223.3 31.2 %copy-start.38 = (s32[640]{0:T(1024)S(1)}, s32[640]{0:T(1024)}, u32[]{:S(2)}) copy-start(s32[640]{0:T(1024)} %copy-done.37) | copy-start | bytes 7684
  223.3 31.2 %copy-start.40 = (s32[640]{0:T(1024)S(1)}, s32[640]{0:T(1024)}, u32[]{:S(2)}) copy-start(s32[640]{0:T(1024)} %copy-done.39) | copy-start | bytes 7684
  223.3 31.2 %copy-start.42 = (s32[640]{0:T(1024)S(1)}, s32[640]{0:T(1024)}, u32[]{:S(2)}) copy-start(s32[640]{0:T(1024)} %copy-done.41) | copy-start | bytes 7684
  223.3 31.2 %copy-start.44 = (s32[640]{0:T(1024)S(1)}, s32[640]{0:T(1024)}, u32[]{:S(2)}) copy-start(s32[640]{0:T(1024)} %copy-done.43) | copy-start | bytes 7684
  223.3 31.2 %copy-start.46 = (s32[640]{0:T(1024)S(1)}, s32[640]{0:T(1024)}, u32[]{:S(2)}) copy-start(s32[640]{0:T(1024)} %copy-done.45) | copy-start | bytes 7684
  223.3 31.2 %copy-start.48 = (s32[640]{0:T(1024)S(1)}, s32[640]{0:T(1024)}, u32[]{:S(2)}) copy-start(s32[640]{0:T(1024)} %copy-done.47) | copy-start | bytes 7684
  223.3 31.2 %copy-start.59 = (pred[640]{0:T(1024)(128)(4,1)S(1)}, pred[640]{0:T(1024)(128)(4,1)}, u32[]{:S(2)}) copy-start(pred[640]{0:T(1024)(128)(4,1)} %copy-done.58) | copy-start | bytes 1924
  223.4 31.2 %copy-start.61 = (pred[640]{0:T(1024)(128)(4,1)S(1)}, pred[640]{0:T(1024)(128)(4,1)}, u32[]{:S(2)}) copy-start(pred[640]{0:T(1024)(128)(4,1)} %copy-done.60) | copy-start | bytes 1924
  223.4 31.2 %copy-start.63 = (pred[640]{0:T(1024)(128)(4,1)S(1)}, pred[640]{0:T(1024)(128)(4,1)}, u32[]{:S(2)}) copy-start(pred[640]{0:T(1024)(128)(4,1)} %copy-done.62) | copy-start | bytes 1924
  223.4 31.2 %copy-start.65 = (pred[640]{0:T(1024)(128)(4,1)S(1)}, pred[640]{0:T(1024)(128)(4,1)}, u32[]{:S(2)}) copy-start(pred[640]{0:T(1024)(128)(4,1)} %copy-done.64) | copy-start | bytes 1924
  254.6 9.3 %slice-start = ((s8[5898240]{0:T(1024)(128)(4,1)}), s8[4194304]{0:T(1024)(128)(4,1)S(1)}, s32[]{:S(2)}) async-start(s8[5898240]{0:T(1024)(128)(4,1)} %bitcast.314), calls=%async_computation.12 | async-start | bytes 8388608
  258.6 5.4 %slice-start.1 = ((s8[5898240]{0:T(1024)(128)(4,1)}), s8[1703936]{0:T(1024)(128)(4,1)S(1)}, s32[]{:S(2)}) async-start(s8[5898240]{0:T(1024)(128)(4,1)} %bitcast.314), calls=%async_computation.13 | async-start | bytes 3407872
  266.0 14.5 %all-to-all-start.4 = ((bf16[4,160,512]{2,1,0:T(8,128)(2,1)}), bf16[4,160,512]{2,1,0:T(8,128)(2,1)}, u32[]{:S(2)}, u32[]{:S(2)}) async-start(bf16[4,160,512]{2,1,0:T(8,128)(2,1)} %fusion.33), calls=%async_computation.5 | async-start | bytes 1310720 | tf_op jit(solution)/shard_map/all_to_all | solution.py:37
  270.2 86.4 %reduce-scatter.5.cloned.1.call-start = ((), (), s32[]{:S(2)}) async-start(), calls=%async_computation.9 | async-start | bytes 1658880 | tf_op jit(solution)/shard_map/reduce_scatter | solution.py:174
  297.7 25.9 %all-to-all-start.5 = ((bf16[32,20,720]{2,1,0:T(8,128)(2,1)}), bf16[32,20,720]{2,1,0:T(8,128)(2,1)}, u32[]{:S(2)}, u32[]{:S(2)}) async-start(bf16[32,20,720]{2,1,0:T(8,128)(2,1)} %reshape.408), calls=%async_computation.6 | async-start | bytes 2359296 | tf_op jit(solution)/shard_map/all_to_all | solution.py:169
  302.4 6.2 %copy-start.1 = (bf16[640,720]{1,0:T(8,128)(2,1)S(1)}, bf16[640,720]{1,0:T(8,128)(2,1)}, u32[]{:S(2)}) copy-start(bf16[640,720]{1,0:T(8,128)(2,1)} %copy.137) | copy-start | bytes 2764804
  302.4 6.2 %copy-start.3 = (bf16[4,160,512]{2,1,0:T(8,128)(2,1)S(1)}, bf16[4,160,512]{2,1,0:T(8,128)(2,1)}, u32[]{:S(2)}) copy-start(bf16[4,160,512]{2,1,0:T(8,128)(2,1)} %copy-done.2) | copy-start | bytes 1966084
  311.2 45.4 %copy-start.50 = (s32[128]{0:T(128)S(1)}, s32[128]{0:T(128)}, u32[]{:S(2)}) copy-start(s32[128]{0:T(128)} %copy-done.49) | copy-start | bytes 1540
  311.2 45.4 %copy-start.52 = (s32[128]{0:T(128)S(1)}, s32[128]{0:T(128)}, u32[]{:S(2)}) copy-start(s32[128]{0:T(128)} %copy-done.51) | copy-start | bytes 1540
  311.2 45.4 %copy-start.54 = (s32[128]{0:T(128)S(1)}, s32[128]{0:T(128)}, u32[]{:S(2)}) copy-start(s32[128]{0:T(128)} %copy-done.53) | copy-start | bytes 1540
  311.2 45.4 %copy-start.56 = (s32[128]{0:T(128)S(1)}, s32[128]{0:T(128)}, u32[]{:S(2)}) copy-start(s32[128]{0:T(128)} %copy-done.55) | copy-start | bytes 1540
  327.7 31.3 %collective-permute-start.1 = (bf16[90,1152]{1,0:T(8,128)(2,1)}, bf16[90,1152]{1,0:T(8,128)(2,1)}, u32[]{:S(2)}, u32[]{:S(2)}) collective-permute-start(bf16[90,1152]{1,0:T(8,128)(2,1)} %dynamic-slice_bitcast_fusion), channel_id=1, source_target_pairs={{0,64},{64,0},{1,65},{65,1},{2,66},{66,2},{3,67},{67,3},{4,68},{68... | collective-permute-start | bytes 622088 | tf_op jit(solution)/shard_map/ppermute | solution.py:140
  (34 other events, 66.0 us)
Sparse Core Ops, SparseCore 0:
  9.7 29.4 all-gather.7
  41.3 65.0 all-gather.5
  205.8 107.3 reduce-scatter.6
  315.5 41.0 reduce-scatter.4

commit v2 on v1

v2 whole, which is shorter than its diff:
```python
import jax
import jax.numpy as jnp
from jax import lax
from jax.sharding import Mesh, PartitionSpec as P

BF = jnp.bfloat16
F32 = jnp.float32
EXPERT = ("yh", "z", "x")
PLANE = ("z", "x")
WIDTH = ("yl", "c")
COLUMN = ("yh", "yl", "c")
CAP = 5
HALF = 384
PADDED = 96
WPART = 768
XROWS = 24


def dot(a, b, dims):
    return lax.dot_general(a, b, (dims, ((), ())), preferred_element_type=F32)


def bdot(a, b, dims):
    return lax.dot_general(a, b, (dims, ((0,), (0,))), preferred_element_type=F32)


def targets_of(routes_t, experts):
    flat = routes_t.reshape(1, -1)
    pairs = flat.shape[1]
    onehot = (flat == lax.broadcasted_iota(jnp.int32, (experts, pairs), 0)).astype(BF)
    earlier = lax.broadcasted_iota(jnp.int32, (pairs, pairs), 0) < lax.broadcasted_iota(
        jnp.int32, (pairs, pairs), 1
    )
    before = dot(onehot, earlier.astype(BF), ((1,), (0,)))
    place = jnp.sum(before * onehot.astype(F32), axis=0).astype(jnp.int32)
    return place.reshape(routes_t.shape)


def width_sum(partial, mask):
    parts = lax.all_to_all(partial.astype(BF), WIDTH, 0, 0)
    total = jnp.sum(parts.astype(F32), axis=0)
    mine = (total * mask).astype(BF)
    return lax.all_gather(mine, WIDTH)


def pad_cols(a):
    return jnp.pad(a, ((0, 0),) * (a.ndim - 1) + ((0, 2 * HALF - a.shape[-1]),))


def swap_y(a):
    return lax.ppermute(a, "yh", [(0, 1), (1, 0)])


def local(tokens, grad_out, routes, gates, ranks, w_gate, w_up, w_down, delta_in, delta_out):
    yh = lax.axis_index("yh")
    wi = lax.axis_index("yl") * 2 + lax.axis_index("c")
    rows, part = tokens.shape
    local_e, _, rank_max = delta_in.shape
    n_exp = 32
    experts = n_exp * local_e
    slots = experts * CAP
    er = n_exp * CAP
    wr = w_gate.shape[0]
    rest = part - HALF

    d_id = lax.broadcasted_iota(jnp.int32, (part, WPART), 0)
    j_id = lax.broadcasted_iota(jnp.int32, (part, WPART), 1)
    spread = ((d_id // wr == j_id // PADDED) & (d_id % wr == j_id % PADDED)).astype(BF)

    w3 = jnp.stack([pad_cols(w_gate), pad_cols(w_up), pad_cols(w_down.T)], axis=1)
    w3 = jnp.pad(w3, ((0, PADDED - wr), (0, 0), (0, 0)))
    keep = lax.dynamic_slice_in_dim(w3, yh * HALF, HALF, 2).reshape(PADDED, 3 * HALF)
    give = lax.dynamic_slice_in_dim(w3, (1 - yh) * HALF, HALF, 2).reshape(PADDED, 3 * HALF)
    own_w = lax.all_gather(keep, PLANE).reshape(2 * WPART, 3 * HALF)
    far_w = lax.all_gather(swap_y(give), PLANE).reshape(2 * WPART, 3 * HALF)

    place = targets_of(routes.T, experts)
    routes_t, gates_t = routes.T, gates.T
    info = jnp.concatenate([(routes_t * 8 + place).astype(F32), gates_t], axis=0)
    far = swap_y(info)
    info2 = jnp.where(
        yh == 0, jnp.concatenate([info, far], axis=1), jnp.concatenate([far, info], axis=1)
    )
    target = (routes_t // local_e) * XROWS + (routes_t % local_e) * CAP + place
    slot_ids = lax.broadcasted_iota(jnp.int32, (n_exp * XROWS, rows), 0)
    picker = sum((target[k : k + 1] == slot_ids).astype(F32) for k in range(4)).astype(BF)

    out_x = dot(picker, tokens, ((1,), (0,))).astype(BF).reshape(n_exp, XROWS, part)
    in_x = lax.all_to_all(out_x, EXPERT, 0, 0).reshape(n_exp * XROWS, part)

    xy = jnp.stack([dot(tokens, spread, ((1,), (0,))), dot(grad_out, spread, ((1,), (0,)))]).astype(BF)
    xy = lax.all_gather(xy, COLUMN).reshape(2, 4, 2, rows, WPART)

    def feats(first, which):
        two = lax.dynamic_slice_in_dim(xy[:, :, which], first, 2, 1)
        return two.transpose(0, 2, 1, 3).reshape(2 * rows, 2 * WPART)

    own_x, far_x, own_y, far_y = [feats(f, k) for k in (0, 1) for f in (2 * yh, 2 - 2 * yh)]

    def order(width, source):
        r = lax.broadcasted_iota(jnp.int32, (slots, width), 0)
        s_in = lax.broadcasted_iota(jnp.int32, (slots, width), 1)
        return (s_in == source(r // er, (r % er) // (2 * CAP), (r % (2 * CAP)) // CAP, r % CAP)).astype(BF)

    perm_x = order(n_exp * XROWS, lambda e, zx, b, p: (b * 16 + zx) * XROWS + e * CAP + p)
    perm_p = order(slots, lambda e, zx, b, p: (zx * 2 + b) * (local_e * CAP) + e * CAP + p)
    rows_x = dot(perm_x, in_x, ((1,), (0,))).astype(BF).reshape(local_e, er, part)
    rank_ids = lax.broadcasted_iota(jnp.int32, (1, rank_max), 1)
    mask = (rank_ids < ranks[wi]).astype(F32)
    low = width_sum(bdot(rows_x, delta_in, ((2,), (1,))), mask)
    halves = []
    for h in range(2):
        cols = []
        for c in range(2):
            d = bdot(low, delta_out[:, :, c, h * HALF : min(part, (h + 1) * HALF)], ((2,), (1,)))
            d = d.astype(BF)
            if h == 1:
                d = jnp.pad(d, ((0, 0), (0, 0), (0, 2 * HALF - part)))
            cols.append(d)
        cols = jnp.concatenate(cols, axis=2).reshape(slots, 2 * HALF)
        halves.append(dot(perm_p, cols, ((0,), (0,))).astype(BF).reshape(16, 2 * local_e * CAP, 2 * HALF))
    back_pre = lax.all_to_all(jnp.concatenate(halves, axis=0), EXPERT, 0, 0)
    back_pre = back_pre.reshape(2 * slots, 2 * HALF)

    coded = info2[:4].astype(jnp.int32)
    route2, place2 = coded // 8, coded % 8
    block2 = lax.broadcasted_iota(jnp.int32, (4, 2 * rows), 1) // rows
    target2 = ((route2 // local_e) * 2 + block2) * (local_e * CAP) + (route2 % local_e) * CAP + place2
    ids2 = lax.broadcasted_iota(jnp.int32, (2 * slots, 2 * rows), 0)
    hits = [target2[k : k + 1] == ids2 for k in range(4)]
    picker2 = sum(h.astype(F32) for h in hits).astype(BF)
    gate_slot = jnp.sum(
        sum(jnp.where(h, info2[4 + k : 5 + k], 0.0) for k, h in enumerate(hits)), axis=1, keepdims=True
    )

    own_gu, own_d, far_gu, far_d = own_w[:, : 2 * HALF], own_w[:, 2 * HALF :], far_w[:, : 2 * HALF], far_w[:, 2 * HALF :]
    base = (dot(own_x, own_gu, ((1,), (0,))) + dot(far_x, far_gu, ((1,), (0,)))).astype(BF)
    down = (dot(own_y, own_d, ((1,), (0,))) + dot(far_y, far_d, ((1,), (0,)))).astype(BF)
    pre = dot(picker2, base, ((1,), (0,))) + back_pre.astype(F32)
    pair_down = (gate_slot * dot(picker2, down, ((1,), (0,)))).astype(BF).astype(F32)
    act, up = pre[:, :HALF], pre[:, HALF:]
    sig = jax.nn.sigmoid(act)
    swish = act * sig
    weighted = (gate_slot * (swish * up)).astype(BF)
    grad_act = pair_down * up * sig * (1.0 + act * (1.0 - sig))
    grad_up_ = pair_down * swish
    pair_grad = jnp.concatenate([grad_act, grad_up_], axis=1).astype(BF)
    in_p = lax.all_to_all(pair_grad.reshape(n_exp, 2 * local_e * CAP, 2 * HALF), EXPERT, 0, 0)
    in_p = in_p.reshape(2, slots, 2 * HALF)
    mixed = dot(picker2, weighted, ((0,), (0,))).astype(BF)
    summed = dot(picker2, pair_grad, ((0,), (0,))).astype(BF)

    def plane_sum(feat, grad):
        dw = dot(feat, grad, ((0,), (0,))).astype(BF)
        return lax.psum_scatter(dw.reshape(16, PADDED, -1), PLANE)

    other_x, other_y = plane_sum(far_x, summed), plane_sum(far_y, mixed)
    mine_x, mine_y = plane_sum(own_x, summed), plane_sum(own_y, mixed)
    other = swap_y(jnp.concatenate([other_x, other_y], axis=1))
    mine = jnp.concatenate([mine_x, mine_y], axis=1)
    lo = jnp.where(yh == 0, mine, other)[:wr]
    hi = jnp.where(yh == 0, other, mine)[:wr]
    grads = [
        jnp.concatenate([lo[:, i * HALF : (i + 1) * HALF], hi[:, i * HALF : i * HALF + rest]], axis=1)
        for i in range(3)
    ]

    dx_own, dx_far = [dot(summed, w, ((1,), (1,))).astype(BF) for w in (own_gu, far_gu)]
    dx = jnp.stack([jnp.where(yh == 0, dx_own, dx_far), jnp.where(yh == 0, dx_far, dx_own)])
    dx = dx.reshape(2, 2, rows, 2, WPART).transpose(1, 0, 3, 2, 4).reshape(8, rows, WPART)
    dx = jnp.sum(lax.all_to_all(dx, COLUMN, 0, 0).astype(F32), axis=0)
    dx_hi = dx.astype(BF)
    dx_lo = (dx - dx_hi.astype(F32)).astype(BF)
    token_grad = dot(dx_hi, spread, ((1,), (1,))) + dot(dx_lo, spread, ((1,), (1,)))

    pg = [dot(perm_p, in_p[h], ((1,), (0,))).astype(BF) for h in range(2)]
    pg = jnp.stack(
        [
            jnp.concatenate([pg[0][:, c * HALF : (c + 1) * HALF], pg[1][:, c * HALF : c * HALF + rest]], axis=1)
            for c in range(2)
        ],
        axis=1,
    ).reshape(local_e, er, 2, part)
    low_back = lax.dot_general(
        pg, delta_out, (((2, 3), (2, 3)), ((0,), (0,))), preferred_element_type=F32
    )
    low_grad = width_sum(low_back, mask)
    grad_delta_out = lax.dot_general(
        low, pg, (((1,), (1,)), ((0,), (0,))), preferred_element_type=F32
    ).astype(BF)
    grad_delta_in = bdot(rows_x, low_grad, ((1,), (1,))).astype(BF)
    back = bdot(low_grad, delta_in, ((2,), (2,))).astype(BF).reshape(slots, part)
    back = dot(perm_x, back, ((0,), (0,))).astype(BF).reshape(n_exp, XROWS, part)
    back = lax.all_to_all(back, EXPERT, 0, 0).reshape(n_exp * XROWS, part)
    grad_tokens = (token_grad + dot(picker, back, ((0,), (0,)))).astype(BF)
    return (grad_tokens, grads[0], grads[1], grads[2].T, grad_delta_in, grad_delta_out)


def solution(mesh):
    fine = Mesh(mesh.devices.reshape(2, 4, 4, 2, 2), ("yh", "z", "x", "yl", "c"))
    return jax.shard_map(
        local,
        mesh=fine,
        in_specs=(
            P(EXPERT, WIDTH),
            P(EXPERT, WIDTH),
            P(EXPERT, None),
            P(EXPERT, None),
            P(EXPERT),
            P(EXPERT, WIDTH),
            P(EXPERT, WIDTH),
            P(WIDTH, EXPERT),
            P(EXPERT, WIDTH, None),
            P(EXPERT, None, None, WIDTH),
        ),
        out_specs=(
            P(EXPERT, WIDTH),
            P(EXPERT, WIDTH),
            P(EXPERT, WIDTH),
            P(WIDTH, EXPERT),
            P(EXPERT, WIDTH, None),
            P(EXPERT, None, None, WIDTH),
        ),
        check_vma=False,
    )
```

time: 376 us -> 520 us (1.38)
  waiting for transfers between devices: 99.4 us -> 286 us
  local copies, waits for them, and re-layouts: 66.4 us -> 37.8 us
  blocking collectives: 31 us -> 14.7 us
    unnamed x5 -> x11, waiting for transfers between devices: 0.07 us -> 189 us
    reshape x7 -> x1, local copies, waits for them, and re-layouts: 30.7 us -> 0.73 us  [local(): lax.dynamic_slice_in_dim(w3, (1 - yh) * HALF, HALF, 2)]
    all_gather x2 -> x3, waiting for transfers between devices: 0.04 us -> 28.8 us  [the longest x1 28.7 us: local(): far_w = lax.all_gather(swap_y(give), PLANE).reshape(2 * WPART, 3 * HALF)]
    reduce_scatter x1 -> x0, waiting for transfers between devices: 27.3 us -> none  [local(): dx = lax.psum_scatter(dx, COLUMN).astype(F32)]
    all_to_all x3 -> x4, waiting for transfers between devices: 61.4 us -> 36.3 us  [the longest x1 18.8 us: local(): in_x = lax.all_to_all(out_x, EXPERT, 0, 0).reshape(n_exp * XROWS, part)]
    all_to_all x1, waiting for transfers between devices: 0.12 us -> 17.2 us  [local(): back_pre = lax.all_to_all(jnp.concatenate(halves, axis=0), EXPERT, 0, 0)]
    all_gather x2 -> x0, blocking collectives: 15.5 us -> none  [the longest x1 9.66 us: local(): target2 = lax.all_gather(target, 'yh')]
    transpose x3 -> x0, local copies, waits for them, and re-layouts: 13.4 us -> none  [the longest x1 6.75 us: local(): full = full.transpose(1, 0, 2, 3).reshape(4, part, 3 * HALF)]
  transfers between devices with their start and end apart: 12 -> 17, of which waited for: 7 -> 10; matrix products, arithmetic and copies ran while one was open for 33% -> 25% of each run, Pallas kernels for 0% -> 0%
where the time goes in v2:
time: 520 us; the launch traced here: 512 us
  waiting for transfers between devices  286 us (55%)
  matrix products  91.1 us (18%)
  starting transfers between devices  46.7 us (9%)
  local copies, waits for them, and re-layouts  37.8 us (7%)
  other arithmetic  20.2 us (4%)
  between operations  15.4 us (3%)
  blocking collectives  14.7 us (3%)
    unnamed x11, waiting for transfers between devices  189 us
    dot_general x25, matrix products, dot(): return lax.dot_general(a, b, (dims, ((), ())), preferred_element_type=F32)  68.6 us
    all_gather x1, waiting for transfers between devices, local(): far_w = lax.all_gather(swap_y(give), PLANE).reshape(2 * WPART, 3 * HALF)  28.7 us
    all_to_all x1, waiting for transfers between devices, local(): in_x = lax.all_to_all(out_x, EXPERT, 0, 0).reshape(n_exp * XROWS, part)  18.8 us
    all_to_all x1, waiting for transfers between devices, local(): back_pre = lax.all_to_all(jnp.concatenate(halves, axis=0), EXPERT, 0, 0)  17.2 us
    all_to_all x2, waiting for transfers between devices, width_sum(): parts = lax.all_to_all(partial.astype(BF), WIDTH, 0, 0)  15.2 us
    dot_general x7, matrix products, bdot(): lax.dot_general(a, b, (dims, ((0,), (0,))), preferred_element_type=F32)  14.9 us
    all_gather x2, blocking collectives, width_sum(): return lax.all_gather(mine, WIDTH)  14.7 us
  transfers between devices with their start and end apart: 17, of which 10 were waited for; matrix products, arithmetic and copies ran while one was open for 25% of the time, Pallas kernels for 0%

profile of v2, /device:TPU:0, one launch (start us, length us, event | category | flops | bytes accessed | tf_op | source)
XLA Modules:
  0.0 512.5 jit_solution(5950790043056557242)
XLA Ops:
  15.3 3.3 collective-permute-start.1
  19.5 2.4 convolution_convert_fusion.9
  21.9 2.4 copy.66
  24.3 8.3 %all-to-all-start = ((bf16[32,24,720]{2,1,0:T(8,128)(2,1)}), bf16[32,24,720]{2,1,0:T(8,128)(2,1)}, u32[]{:S(2)}, u32[]{:S(2)}) async-start(bf16[32,24,720]{2,1,0:T(8,128)(2,1)} %bitcast.216), calls=%async_computation | async-start | bytes 2359296 | tf_op jit(solution)/shard_map/all_to_all | solution.py:89
  34.9 18.8 %all-to-all-done = bf16[32,24,720]{2,1,0:T(8,128)(2,1)} async-done(((bf16[32,24,720]{2,1,0:T(8,128)(2,1)}), bf16[32,24,720]{2,1,0:T(8,128)(2,1)}, u32[]{:S(2)}, u32[]{:S(2)}) %all-to-all-start) | async-done | bytes 1105952 | tf_op jit(solution)/shard_map/all_to_all | solution.py:89
  53.7 3.3 convolution_convert_fusion.15
  56.9 2.2 copy.67
  59.2 2.7 convolution_convert_fusion.16
  61.9 4.2 all-to-all-start.1
  67.9 8.5 %all-to-all-done.1 = bf16[4,160,512]{2,1,0:T(8,128)(2,1)} async-done(((bf16[4,160,512]{2,1,0:T(8,128)(2,1)}), bf16[4,160,512]{2,1,0:T(8,128)(2,1)}, u32[]{:S(2)}, u32[]{:S(2)}) %all-to-all-start.1) | async-done | bytes 655392 | tf_op jit(solution)/shard_map/all_to_all | solution.py:40
  77.7 7.4 %all_gather.25 = bf16[4,160,512]{2,1,0:T(8,128)(2,1)S(1)} all-gather(bf16[1,160,512]{2,1,0:T(8,128)(2,1)S(1)} %fusion.97), channel_id=1, replica_groups=mesh['yh'=2,'z'=4,'x'=4,'yl'=2,'c'=2] {'yl','c'}, dimensions={0}, use_global_device_ids=true | all-gather | bytes 819200 | tf_op jit(solution)/shard_map/all_gather | solution.py:43
  87.4 2.2 fusion.56
  99.6 5.5 %all-to-all-start.2 = ((bf16[32,40,768]{2,1,0:T(8,128)(2,1)}), bf16[32,40,768]{2,1,0:T(8,128)(2,1)}, u32[]{:S(2)}, u32[]{:S(2)}) async-start(bf16[32,40,768]{2,1,0:T(8,128)(2,1)} %pad_maximum_fusion), calls=%async_computation.2 | async-start | bytes 3932160 | tf_op jit(solution)/shard_map/all_to_all | solution.py:122
  114.8 3.6 fusion.7
  118.4 17.2 %all-to-all-done.2 = bf16[32,40,768]{2,1,0:T(8,128)(2,1)} async-done(((bf16[32,40,768]{2,1,0:T(8,128)(2,1)}), bf16[32,40,768]{2,1,0:T(8,128)(2,1)}, u32[]{:S(2)}, u32[]{:S(2)}) %all-to-all-start.2) | async-done | bytes 1966112 | tf_op jit(solution)/shard_map/all_to_all | solution.py:122
  135.6 28.7 %all-gather.9.cloned.1.call-done = bf16[1536,1152]{1,0:T(8,128)(2,1)} async-done(((bf16[96,1152]{1,0:T(8,128)(2,1)}), bf16[1536,1152]{1,0:T(8,128)(2,1)}) %all-gather.9.cloned.1.call-update) | async-done | bytes 3538960 | tf_op jit(solution)/shard_map/all_gather | solution.py:75
  164.3 6.3 %convolution_add_fusion = f32[1280,768]{1,0:T(8,128)} fusion(bf16[1280,768]{1,0:T(8,128)(2,1)} %bitcast.82, f32[256,768]{1,0:T(8,128)} %fusion.7, bf16[256,1536]{1,0:T(8,128)(2,1)} %bitcast.224, bf16[1536,1152]{1,0:T(8,128)(2,1)} %all-gather.9.cloned.1.call-done, s32[256]{0:T(256)S(1)} %bitcast.257, s32[256]{0:T(256)S(1)} %bitcast.262, s32[256]{0:T(256)S(1)} %bitcast.267, ...), kind=kOutput, calls=%fused_computation | convolution fusion | flops 1113587712 | bytes 9834496 | tf_op jit(solution)/shard_map/dot_general | solution.py:20
  170.6 3.6 convolution_convert_fusion.17
  179.3 2.6 fusion.77
  181.9 6.3 %multiply_convert_fusion.2 = (bf16[1280,384]{1,0:T(8,128)(2,1)}, bf16[1280,384]{1,0:T(8,128)(2,1)}) fusion(f32[1280,768]{1,0:T(8,128)} %convolution_add_fusion, f32[256,384]{1,0:T(8,128)} %fusion.77, bf16[256,1536]{1,0:T(8,128)(2,1)} %bitcast.227, bf16[1536,1152]{1,0:T(8,128)(2,1)} %all-gather.9.cloned.1.call-done, s32[256]{0:T(256)S(1)} %bitcast.259, ...), kind=kOutput, calls=%fused_computation.58 | convolution fusion | flops 565641216 | bytes 8266752 | tf_op jit(solution)/shard_map/dot_general | solution.py:20
  188.2 2.5 fusion.71
  190.8 2.3 convolution_convert_fusion
  193.1 2.8 convolution_convert_fusion.4
  195.9 3.0 pad_maximum_fusion.1
  198.9 7.4 %all-to-all-start.4 = ((bf16[32,40,768]{2,1,0:T(8,128)(2,1)}), bf16[32,40,768]{2,1,0:T(8,128)(2,1)}, u32[]{:S(2)}, u32[]{:S(2)}) async-start(bf16[32,40,768]{2,1,0:T(8,128)(2,1)} %pad_maximum_fusion.1), calls=%async_computation.4 | async-start | bytes 3932160 | tf_op jit(solution)/shard_map/all_to_all | solution.py:148
  206.4 2.7 convolution_convert_fusion.6
  211.1 3.0 stack.46
  216.2 2.9 stack.47
  223.6 2.7 pad_maximum_fusion.3
  226.2 9.2 %all-to-all-done.4 = bf16[32,40,768]{2,1,0:T(8,128)(2,1)} async-done(((bf16[32,40,768]{2,1,0:T(8,128)(2,1)}), bf16[32,40,768]{2,1,0:T(8,128)(2,1)}, u32[]{:S(2)}, u32[]{:S(2)}) %all-to-all-start.4) | async-done | bytes 1966112 | tf_op jit(solution)/shard_map/all_to_all | solution.py:148
  235.5 4.5 all-to-all-start.3
  241.8 3.8 convolution_convert_fusion.12
  245.7 3.8 convolution_convert_fusion.11
  253.2 8.3 %all-to-all-done.3 = bf16[8,128,768]{2,1,0:T(8,128)(2,1)} async-done(((bf16[8,128,768]{2,1,0:T(8,128)(2,1)}), bf16[8,128,768]{2,1,0:T(8,128)(2,1)}, u32[]{:S(2)}, u32[]{:S(2)}) %all-to-all-start.3) | async-done | bytes 1572896 | tf_op jit(solution)/shard_map/all_to_all | solution.py:171
  261.5 4.2 all-to-all-start.5
  269.4 6.7 %all-to-all-done.5 = bf16[4,160,512]{2,1,0:T(8,128)(2,1)} async-done(((bf16[4,160,512]{2,1,0:T(8,128)(2,1)}), bf16[4,160,512]{2,1,0:T(8,128)(2,1)}, u32[]{:S(2)}, u32[]{:S(2)}) %all-to-all-start.5) | async-done | bytes 655392 | tf_op jit(solution)/shard_map/all_to_all | solution.py:40
  277.3 7.3 %all_gather.26 = bf16[4,160,512]{2,1,0:T(8,128)(2,1)S(1)} all-gather(bf16[1,160,512]{2,1,0:T(8,128)(2,1)S(1)} %fusion.96), channel_id=1, replica_groups=mesh['yh'=2,'z'=4,'x'=4,'yl'=2,'c'=2] {'yl','c'}, dimensions={0}, use_global_device_ids=true | all-gather | bytes 819200 | tf_op jit(solution)/shard_map/all_gather | solution.py:43
  285.6 3.0 convolution_convert_fusion.8
  288.7 2.4 copy.76
  291.0 4.9 all-to-all-start.6
  296.0 2.6 convolution_add_fusion.3
  298.6 5.6 %convolution_convert_fusion.2 = bf16[4,512,2,720]{1,3,2,0:T(8,128)(2,1)} fusion(bf16[4,160,1,720]{3,1,2,0:T(8,128)(2,1)S(1)} %bitcast.221, bf16[4,160,1,720]{3,1,2,0:T(8,128)(2,1)S(1)} %bitcast.219, bf16[4,160,512]{2,1,0:T(8,128)(2,1)} %copy-done.12), kind=kOutput, calls=%fused_computation.9 | convolution fusion | flops 950353920 | bytes 8396800 | tf_op jit(solution)/shard_map/dot_general | solution.py:188
  304.2 2.6 convolution_convert_fusion.7
  306.8 42.2 %reduce-scatter.17.cloned.1.call-done = bf16[1,96,768]{2,1,0:T(8,128)(2,1)} async-done(((bf16[16,96,768]{2,1,0:T(8,128)(2,1)}), bf16[1,96,768]{2,1,0:T(8,128)(2,1)}) %reduce-scatter.17.cloned.1.call-update) | async-done | bytes 147472
  350.0 3.0 collective-permute-start.2
  353.1 2.6 fusion.82
  355.7 68.9 %reduce-scatter.15.cloned.1.call-done = bf16[1,96,384]{2,1,0:T(8,128)(2,1)} async-done(((bf16[16,96,384]{2,1,0:T(8,128)(2,1)}), bf16[1,96,384]{2,1,0:T(8,128)(2,1)}) %reduce-scatter.15.cloned.1.call-update) | async-done | bytes 73744
  424.6 77.7 %reduce-scatter.13.cloned.1.call-done = bf16[1,96,768]{2,1,0:T(8,128)(2,1)} async-done(((bf16[16,96,768]{2,1,0:T(8,128)(2,1)}), bf16[1,96,768]{2,1,0:T(8,128)(2,1)}) %reduce-scatter.13.cloned.1.call-update) | async-done | bytes 147472
  (213 shorter events, 64.8 us)
Async XLA Ops:
  7.2 52.0 %copy-start = (bf16[4,720,512]{2,1,0:T(8,128)(2,1)S(1)}, bf16[4,720,512]{2,1,0:T(8,128)(2,1)}, u32[]{:S(2)}) copy-start(bf16[4,720,512]{2,1,0:T(8,128)(2,1)} %param.18) | copy-start | bytes 8847364
  7.2 3.2 copy-start.16
  7.2 98.9 %all-gather.5.cloned.1.call-start = ((), (), s32[]{:S(2)}) async-start(), calls=%async_computation.11 | async-start | bytes 3538944 | tf_op jit(solution)/shard_map/all_gather | solution.py:92
  8.4 2.9 copy-start.13
  12.3 102.5 %all-gather.7.cloned.1.call-start = ((), (), s32[]{:S(2)}) async-start(), calls=%async_computation.12 | async-start | bytes 3760128 | tf_op jit(solution)/shard_map/all_gather | solution.py:74
  13.4 5.2 %copy-start.49 = (s32[128,4]{0,1:T(4,128)S(1)}, s32[128,4]{0,1:T(4,128)}, u32[]{:S(2)}) copy-start(s32[128,4]{0,1:T(4,128)} %param.12) | copy-start | bytes 6148
  15.3 19.5 %collective-permute-start.1 = (bf16[96,1152]{1,0:T(8,128)(2,1)}, bf16[96,1152]{1,0:T(8,128)(2,1)}, u32[]{:S(2)}, u32[]{:S(2)}) collective-permute-start(bf16[96,1152]{1,0:T(8,128)(2,1)} %bitcast.95), channel_id=1, source_target_pairs={{0,64},{64,0},{1,65},{65,1},{2,66},{66,2},{3,67},{67,3},{4,68},{68... | collective-permute-start | bytes 663560 | tf_op jit(solution)/shard_map/ppermute | solution.py:51
  24.3 29.4 %all-to-all-start = ((bf16[32,24,720]{2,1,0:T(8,128)(2,1)}), bf16[32,24,720]{2,1,0:T(8,128)(2,1)}, u32[]{:S(2)}, u32[]{:S(2)}) async-start(bf16[32,24,720]{2,1,0:T(8,128)(2,1)} %bitcast.216), calls=%async_computation | async-start | bytes 2359296 | tf_op jit(solution)/shard_map/all_to_all | solution.py:89
  32.6 131.8 %all-gather.9.cloned.1.call-start = ((), (), s32[]{:S(2)}) async-start(), calls=%async_computation.13 | async-start | bytes 3760128 | tf_op jit(solution)/shard_map/all_gather | solution.py:75
  32.6 63.4 %copy-start.29 = (pred[640]{0:T(1024)(128)(4,1)}, pred[640]{0:T(1024)(128)(4,1)S(1)}, u32[]{:S(2)}) copy-start(pred[640]{0:T(1024)(128)(4,1)S(1)} %get-tuple-element.68) | copy-start | bytes 1924
  32.6 63.4 %copy-start.31 = (pred[640]{0:T(1024)(128)(4,1)}, pred[640]{0:T(1024)(128)(4,1)S(1)}, u32[]{:S(2)}) copy-start(pred[640]{0:T(1024)(128)(4,1)S(1)} %get-tuple-element.69) | copy-start | bytes 1924
  32.7 63.4 %copy-start.18 = (s32[640]{0:T(1024)}, s32[640]{0:T(1024)S(1)}, u32[]{:S(2)}) copy-start(s32[640]{0:T(1024)S(1)} %get-tuple-element.63) | copy-start | bytes 7684
  32.7 63.3 %copy-start.20 = (s32[640]{0:T(1024)}, s32[640]{0:T(1024)S(1)}, u32[]{:S(2)}) copy-start(s32[640]{0:T(1024)S(1)} %get-tuple-element.60) | copy-start | bytes 7684
  32.7 63.3 %copy-start.22 = (s32[640]{0:T(1024)}, s32[640]{0:T(1024)S(1)}, u32[]{:S(2)}) copy-start(s32[640]{0:T(1024)S(1)} %get-tuple-element.61) | copy-start | bytes 7684
  32.7 63.3 %copy-start.33 = (pred[640]{0:T(1024)(128)(4,1)}, pred[640]{0:T(1024)(128)(4,1)S(1)}, u32[]{:S(2)}) copy-start(pred[640]{0:T(1024)(128)(4,1)S(1)} %get-tuple-element.66) | copy-start | bytes 1924
  32.7 63.3 %copy-start.35 = (pred[640]{0:T(1024)(128)(4,1)}, pred[640]{0:T(1024)(128)(4,1)S(1)}, u32[]{:S(2)}) copy-start(pred[640]{0:T(1024)(128)(4,1)S(1)} %get-tuple-element.67) | copy-start | bytes 1924
  32.8 63.3 %copy-start.24 = (s32[640]{0:T(1024)}, s32[640]{0:T(1024)S(1)}, u32[]{:S(2)}) copy-start(s32[640]{0:T(1024)S(1)} %get-tuple-element.58) | copy-start | bytes 7684
  32.8 63.3 %copy-start.26 = (s32[640]{0:T(1024)}, s32[640]{0:T(1024)S(1)}, u32[]{:S(2)}) copy-start(s32[640]{0:T(1024)S(1)} %get-tuple-element.59) | copy-start | bytes 7684
  59.2 6.9 %copy-start.28 = (f32[128,4]{0,1:T(4,128)S(1)}, f32[128,4]{0,1:T(4,128)}, u32[]{:S(2)}) copy-start(f32[128,4]{0,1:T(4,128)} %param.13) | copy-start | bytes 6148
  59.2 7.5 %copy-start.51 = (s32[4]{0:T(128)S(1)}, s32[4]{0:T(128)}, u32[]{:S(2)}) copy-start(s32[4]{0:T(128)} %param.14) | copy-start | bytes 52
  61.9 14.5 %all-to-all-start.1 = ((bf16[4,160,512]{2,1,0:T(8,128)(2,1)}), bf16[4,160,512]{2,1,0:T(8,128)(2,1)}, u32[]{:S(2)}, u32[]{:S(2)}) async-start(bf16[4,160,512]{2,1,0:T(8,128)(2,1)} %convolution_convert_fusion.16), calls=%async_computation.1 | async-start | bytes 1310720 | tf_op jit(solution)/shard_map/all_to_all | solution.py:40
  66.1 39.2 %collective-permute-start = (f32[8,128]{1,0:T(8,128)S(1)}, f32[8,128]{1,0:T(8,128)S(1)}, u32[]{:S(2)}, u32[]{:S(2)}) collective-permute-start(f32[8,128]{1,0:T(8,128)S(1)} %pad_maximum_fusion.14), channel_id=1, source_target_pairs={{0,64},{64,0},{1,65},{65,1},{2,66},{66,2},{3,67},{67,3},{4,68},{68... | collective-permute-start | bytes 12296 | tf_op jit(solution)/shard_map/ppermute | solution.py:51
  85.1 6.6 %copy-start.12 = (bf16[4,160,512]{2,1,0:T(8,128)(2,1)}, bf16[4,160,512]{2,1,0:T(8,128)(2,1)S(1)}, u32[]{:S(2)}) copy-start(bf16[4,160,512]{2,1,0:T(8,128)(2,1)S(1)} %all_gather.25) | copy-start | bytes 1966084
  99.6 36.0 %all-to-all-start.2 = ((bf16[32,40,768]{2,1,0:T(8,128)(2,1)}), bf16[32,40,768]{2,1,0:T(8,128)(2,1)}, u32[]{:S(2)}, u32[]{:S(2)}) async-start(bf16[32,40,768]{2,1,0:T(8,128)(2,1)} %pad_maximum_fusion), calls=%async_computation.2 | async-start | bytes 3932160 | tf_op jit(solution)/shard_map/all_to_all | solution.py:122
  105.1 201.7 %reduce-scatter.19.cloned.1.call-start = ((), (), s32[]{:S(2)}) async-start(), calls=%async_computation.17 | async-start | bytes 1253376
  105.5 76.5 %copy-start.37 = (s32[1,256]{1,0:T(1,128)}, s32[1,256]{1,0:T(1,128)S(1)}, u32[]{:S(2)}) copy-start(s32[1,256]{1,0:T(1,128)S(1)} %get-tuple-element.38) | copy-start | bytes 3076
  105.5 76.5 %copy-start.38 = (s32[1,256]{1,0:T(1,128)}, s32[1,256]{1,0:T(1,128)S(1)}, u32[]{:S(2)}) copy-start(s32[1,256]{1,0:T(1,128)S(1)} %get-tuple-element.39) | copy-start | bytes 3076
  105.5 76.5 %copy-start.39 = (s32[1,256]{1,0:T(1,128)}, s32[1,256]{1,0:T(1,128)S(1)}, u32[]{:S(2)}) copy-start(s32[1,256]{1,0:T(1,128)S(1)} %get-tuple-element.40) | copy-start | bytes 3076
  105.5 76.5 %copy-start.40 = (s32[1,256]{1,0:T(1,128)}, s32[1,256]{1,0:T(1,128)S(1)}, u32[]{:S(2)}) copy-start(s32[1,256]{1,0:T(1,128)S(1)} %get-tuple-element.41) | copy-start | bytes 3076
  170.6 3.6 copy-start.10
  176.0 173.1 %reduce-scatter.17.cloned.1.call-start = ((), (), s32[]{:S(2)}) async-start(), calls=%async_computation.16 | async-start | bytes 2506752
  193.1 231.5 %reduce-scatter.15.cloned.1.call-start = ((), (), s32[]{:S(2)}) async-start(), calls=%async_computation.15 | async-start | bytes 1253376
  198.9 36.6 %all-to-all-start.4 = ((bf16[32,40,768]{2,1,0:T(8,128)(2,1)}), bf16[32,40,768]{2,1,0:T(8,128)(2,1)}, u32[]{:S(2)}, u32[]{:S(2)}) async-start(bf16[32,40,768]{2,1,0:T(8,128)(2,1)} %pad_maximum_fusion.1), calls=%async_computation.4 | async-start | bytes 3932160 | tf_op jit(solution)/shard_map/all_to_all | solution.py:148
  206.3 296.0 %reduce-scatter.13.cloned.1.call-start = ((), (), s32[]{:S(2)}) async-start(), calls=%async_computation.14 | async-start | bytes 2506752
  206.3 2.8 copy-start.50
  235.5 26.1 %all-to-all-start.3 = ((bf16[8,128,768]{2,1,0:T(8,128)(2,1)}), bf16[8,128,768]{2,1,0:T(8,128)(2,1)}, u32[]{:S(2)}, u32[]{:S(2)}) async-start(bf16[8,128,768]{2,1,0:T(8,128)(2,1)} %bitcast.213), calls=%async_computation.3 | async-start | bytes 3145728 | tf_op jit(solution)/shard_map/all_to_all | solution.py:171
  241.8 9.4 %slice-start = ((s8[5898240]{0:T(1024)(128)(4,1)}), s8[4194304]{0:T(1024)(128)(4,1)S(1)}, s32[]{:S(2)}) async-start(s8[5898240]{0:T(1024)(128)(4,1)} %bitcast.276), calls=%async_computation.18 | async-start | bytes 8388608
  245.6 5.5 %slice-start.1 = ((s8[5898240]{0:T(1024)(128)(4,1)}), s8[1703936]{0:T(1024)(128)(4,1)S(1)}, s32[]{:S(2)}) async-start(s8[5898240]{0:T(1024)(128)(4,1)} %bitcast.276), calls=%async_computation.19 | async-start | bytes 3407872
  253.2 14.9 %copy-start.14 = (pred[720,768]{1,0:T(8,128)(4,1)S(1)}, pred[720,768]{1,0:T(8,128)(4,1)}, u32[]{:S(2)}) copy-start(pred[720,768]{1,0:T(8,128)(4,1)} %copy-done.13) | copy-start | bytes 1658884
  261.5 14.5 %all-to-all-start.5 = ((bf16[4,160,512]{2,1,0:T(8,128)(2,1)}), bf16[4,160,512]{2,1,0:T(8,128)(2,1)}, u32[]{:S(2)}, u32[]{:S(2)}) async-start(bf16[4,160,512]{2,1,0:T(8,128)(2,1)} %fusion.52), calls=%async_computation.5 | async-start | bytes 1310720 | tf_op jit(solution)/shard_map/all_to_all | solution.py:40
  291.0 62.0 %all-to-all-start.6 = ((bf16[32,24,720]{2,1,0:T(8,128)(2,1)}), bf16[32,24,720]{2,1,0:T(8,128)(2,1)}, u32[]{:S(2)}, u32[]{:S(2)}) async-start(bf16[32,24,720]{2,1,0:T(8,128)(2,1)} %bitcast.217), calls=%async_computation.6 | async-start | bytes 2359296 | tf_op jit(solution)/shard_map/all_to_all | solution.py:194
  298.6 5.6 %copy-start.1 = (bf16[640,720]{1,0:T(8,128)(2,1)S(1)}, bf16[640,720]{1,0:T(8,128)(2,1)}, u32[]{:S(2)}) copy-start(bf16[640,720]{1,0:T(8,128)(2,1)} %copy.67) | copy-start | bytes 2764804
  298.6 5.6 %copy-start.3 = (bf16[4,160,512]{2,1,0:T(8,128)(2,1)S(1)}, bf16[4,160,512]{2,1,0:T(8,128)(2,1)}, u32[]{:S(2)}) copy-start(bf16[4,160,512]{2,1,0:T(8,128)(2,1)} %copy-done.2) | copy-start | bytes 1966084
  304.2 48.9 %copy-start.42 = (s32[128]{0:T(128)S(1)}, s32[128]{0:T(128)}, u32[]{:S(2)}) copy-start(s32[128]{0:T(128)} %copy-done.41) | copy-start | bytes 1540
  304.2 48.9 %copy-start.44 = (s32[128]{0:T(128)S(1)}, s32[128]{0:T(128)}, u32[]{:S(2)}) copy-start(s32[128]{0:T(128)} %copy-done.43) | copy-start | bytes 1540
  304.2 48.9 %copy-start.46 = (s32[128]{0:T(128)S(1)}, s32[128]{0:T(128)}, u32[]{:S(2)}) copy-start(s32[128]{0:T(128)} %copy-done.45) | copy-start | bytes 1540
  304.2 48.9 %copy-start.48 = (s32[128]{0:T(128)S(1)}, s32[128]{0:T(128)}, u32[]{:S(2)}) copy-start(s32[128]{0:T(128)} %copy-done.47) | copy-start | bytes 1540
  350.0 152.3 %collective-permute-start.2 = (bf16[96,1152]{1,0:T(8,128)(2,1)S(1)}, bf16[96,1152]{1,0:T(8,128)(2,1)S(1)}, u32[]{:S(2)}, u32[]{:S(2)}) collective-permute-start(bf16[96,1152]{1,0:T(8,128)(2,1)S(1)} %pad_maximum_fusion.11), channel_id=1, source_target_pairs={{0,64},{64,0},{1,65},{65,1},{2,66},{66,2},{3,67},{67,3},{4,68},{68... | collective-permute-start | bytes 663560 | tf_op jit(solution)/shard_map/ppermute | solution.py:51
  (23 other events, 34.6 us)
Sparse Core Ops, SparseCore 0:
  12.4 42.8 all-gather.4
  57.4 49.2 all-gather.6
  108.9 55.4 all-gather.8
  176.1 87.3 reduce-scatter.18
  266.6 82.3 reduce-scatter.16
  352.1 72.4 reduce-scatter.14
  427.9 74.3 reduce-scatter.12
